TPU v7x, 256 devices: a whole 4x4x8 slice. The times are simulated.
256 devices in a mesh: dp: 32 (over x, z), tensor: 8 (over y, core).
Axes of the slice: x: 4, y: 4, z: 8, core: 2. Of those that a mesh axis runs over, the one named last changes fastest.
Arguments:
- gradient: bfloat16 [2048, 28672], P('dp', 'tensor')
- owner: int32 [8, 4, 7], P('tensor'), may hold values from 0 to 31, as said below
- prev_left: float32 [8, 32, 512, 512], P('tensor', 'dp'), as said below
- prev_right: float32 [8, 32, 512, 512], P('tensor', 'dp'), as said below
Outputs:
- update: bfloat16 [2048, 28672], P('dp', 'tensor')
- stats_left: float32 [8, 32, 512, 512], P('tensor', 'dp')
- stats_right: float32 [8, 32, 512, 512], P('tensor', 'dp')
Inputs may be any that keep to these rules, and one draw needn't show every extreme that they name: `owner`: in each tensor slice no dp index owns more than 1 block nor two blocks of the same row block i, and some dp index owns exactly 1. `prev_left`: symmetric positive definite. `prev_right`: symmetric positive definite.
All inputs are finite; a program needn't handle non-finite values.
Results may differ from a plain program's by a relative error of at most 0.0071.
Values may be sent and summed in bfloat16 or wider, within the bound.
No kernel may reach another device: no remote copies, remote signals or barrier semaphores. Data moves between devices by JAX's collectives and lax.ppermute only.
A program may use at most 64 MiB of HBM per device.

v0:
```python
import jax
import jax.numpy as jnp
from jax import lax
from jax.sharding import PartitionSpec as P

DECAY = 0.9
EPSILON = 1e-06


def matmul_full(left, right):
    return jnp.einsum(
        "kab,kbc->kac",
        left,
        right,
        precision=lax.Precision.HIGHEST,
        preferred_element_type=jnp.float32,
    )


def inverse_root(stats):
    identity = jnp.eye(stats.shape[1], dtype=jnp.float32)[None]
    frob_norm = jnp.sqrt(jnp.sum(stats * stats, axis=(1, 2), keepdims=True) + EPSILON)
    normed = stats / frob_norm
    step_one = (5.0 * identity - normed) * 0.25
    square = matmul_full(step_one, step_one)
    fourth = matmul_full(square, square)
    updated = matmul_full(fourth, normed)
    step_two = (5.0 * identity - updated) * 0.25
    return matmul_full(step_one, step_two) * frob_norm ** (-0.25)


def body(gradient, owner, prev_left, prev_right):
    shard_rows, slab_cols = gradient.shape
    block_size = prev_left.shape[2]
    col_blocks = slab_cols // block_size
    row_blocks = owner.shape[1]
    owners_dp = lax.axis_size("dp")
    my_index = lax.axis_index("dp")
    owner_table = owner[0]
    owned_flat = (owner_table.reshape(-1) == my_index).astype(jnp.int32)
    order_rank = jnp.cumsum(owned_flat) - 1
    positions = jnp.arange(owned_flat.shape[0], dtype=jnp.int32)
    slot_hit = owned_flat * (order_rank == 0).astype(jnp.int32)
    where_hit = jnp.sum(slot_hit * positions)
    filled = jnp.sum(slot_hit) > 0
    row_start = where_hit // col_blocks * block_size
    col_start = where_hit % col_blocks * block_size
    my_block_row = my_index * shard_rows // block_size
    my_line = lax.dynamic_index_in_dim(owner_table, my_block_row, 0, keepdims=False)
    chooser = (my_line[None, :] == jnp.arange(owners_dp, dtype=jnp.int32)[:, None]).astype(
        jnp.bfloat16
    )
    zero_block = jnp.zeros((block_size, block_size), jnp.bfloat16)
    collected = lax.dynamic_slice_in_dim(
        lax.all_gather(gradient, "dp", axis=0, tiled=True), col_start, block_size, 1
    )
    picked = lax.dynamic_slice(collected, (row_start, 0), (block_size, block_size))
    blocks = jnp.stack([jnp.where(filled, picked, zero_block)])
    grad_local = jnp.sum(jnp.square(gradient.astype(jnp.float32)))
    grad_total = lax.psum(grad_local, ("dp", "tensor"))
    gram_left = (
        jnp.einsum("kab,kcb->kac", blocks, blocks, preferred_element_type=jnp.float32) / block_size
    )
    gram_right = (
        jnp.einsum("kba,kbc->kac", blocks, blocks, preferred_element_type=jnp.float32) / block_size
    )
    stats_left = DECAY * prev_left[0] + (1.0 - DECAY) * gram_left
    stats_right = DECAY * prev_right[0] + (1.0 - DECAY) * gram_right
    root_left = inverse_root(stats_left).astype(jnp.bfloat16)
    root_right = inverse_root(stats_right).astype(jnp.bfloat16)
    half_done = jnp.einsum(
        "kab,kbc->kac", blocks, root_right, preferred_element_type=jnp.float32
    ).astype(jnp.bfloat16)
    conditioned = jnp.einsum(
        "kab,kbc->kac", root_left, half_done, preferred_element_type=jnp.float32
    )
    cond_local = jnp.sum(conditioned * conditioned)
    cond_total = lax.psum(cond_local, ("dp", "tensor"))
    graft_scale = jnp.sqrt(grad_total / (cond_total + EPSILON))
    packed = conditioned.astype(jnp.bfloat16)
    targets = jnp.stack([jnp.where(filled, row_start // block_size, -1)])
    placing = (jnp.arange(row_blocks, dtype=jnp.int32)[:, None] == targets[None, :]).astype(
        jnp.bfloat16
    )
    back_rows = jnp.einsum(
        "rk,kab->rab", placing, packed, preferred_element_type=jnp.float32
    ).astype(jnp.bfloat16)
    returned = lax.all_to_all(
        back_rows.reshape(row_blocks * block_size, block_size),
        "dp",
        split_axis=0,
        concat_axis=0,
        tiled=True,
    )
    returned = returned.reshape(owners_dp, shard_rows, block_size)
    gathered_back = jnp.einsum("oj,ock->cjk", chooser, returned, preferred_element_type=jnp.float32)
    update = (graft_scale * gathered_back).astype(jnp.bfloat16).reshape(shard_rows, slab_cols)
    return (update, stats_left[None], stats_right[None])


def solution(mesh):
    return jax.shard_map(
        body,
        mesh=mesh,
        in_specs=(
            P("dp", "tensor"),
            P("tensor", None, None),
            P("tensor", "dp", None, None),
            P("tensor", "dp", None, None),
        ),
        out_specs=(P("dp", "tensor"), P("tensor", "dp", None, None), P("tensor", "dp", None, None)),
        check_vma=False,
    )
```

profile of v0, /device:TPU:32, one launch (start us, length us, event | category | flops | bytes accessed | tf_op | source)
XLA Modules:
  0.0 280.7 jit_solution(11350962367515250459)
XLA Ops:
  7.2 0.0 all-gather.2.cloned.1.call-start
  7.2 0.7 all-gather.2.cloned.1.call-update
  7.9 0.7 compare_convert_fusion.1
  8.6 0.1 reshape.198
  8.7 0.1 reshape.196
  8.8 0.1 fusion.39
  8.9 0.6 fusion.43
  12.2 129.2 %all-gather.2.cloned.1.call-done = bf16[2048,3584]{1,0:T(8,128)(2,1)} async-done(((bf16[64,3584]{1,0:T(8,128)(2,1)}), bf16[2048,3584]{1,0:T(8,128)(2,1)}) %all-gather.2.cloned.1.call-update) | async-done | bytes 14680080 | tf_op jit(solution)/shard_map/all_gather | solution.py:55
  141.4 3.2 %multiply_reduce_fusion.1 = (f32[]{:T(128)}, f32[512,512]{1,0:T(8,128)S(1)}) fusion(bf16[2048,3584]{1,0:T(8,128)(2,1)} %all-gather.2.cloned.1.call-done, s32[]{:T(128)S(6)} %select_n.46, s32[]{:T(128)S(6)} %select_n.49, pred[]{:T(512)S(6)} %gt.3, f32[1,1,512,512]{3,2,1,0:T(8,128)} %param.7), kind=kOutput, calls=%fused_computation.24 | convolution fusion | flops 270008320 | bytes 2621453 | tf_op jit(solution)/shard_map/kba,kbc->kac/dot_general | solution.py:65
  145.3 2.0 fusion.18
  147.3 0.0 copy-start.1
  147.3 1.8 fusion.61
  149.2 2.9 %fusion.8 = f32[512,512]{1,0:T(8,128)} fusion(f32[512,512]{1,0:T(8,128)S(1)} %fusion.61, f32[512,512]{1,0:T(8,128)S(1)} %get-tuple-element.12, f32[]{:T(128)S(6)} %sqrt.12), kind=kOutput, calls=%fused_computation.15 | convolution fusion | flops 1611923456 | bytes 3145732 | tf_op jit(solution)/shard_map/kab,kbc->kac/dot_general | solution.py:11
  152.1 0.0 copy-done.1
  152.1 2.8 multiply_reduce_fusion.2
  155.7 2.0 fusion.21
  157.7 0.0 copy-start.5
  157.7 1.8 fusion.60
  159.5 1.9 fusion.7
  161.4 0.0 copy-done.2
  161.4 0.0 copy-done.5
  161.4 3.0 %fusion.10 = bf16[512,512]{1,0:T(8,128)(2,1)} fusion(f32[512,512]{1,0:T(8,128)S(1)} %copy-done.5, f32[]{:T(128)S(6)} %pow.9, f32[512,512]{1,0:T(8,128)S(1)} %get-tuple-element.12, f32[]{:T(128)S(6)} %sqrt.12), kind=kOutput, calls=%fused_computation.17 | convolution fusion | flops 1612447744 | bytes 2621448 | tf_op jit(solution)/shard_map/kab,kbc->kac/dot_general | solution.py:11
  164.4 2.0 fusion.9
  166.4 2.7 multiply_reduce_fusion
  169.0 1.9 multiply_convert_fusion
  171.0 7.7 %all-to-all-start = ((bf16[32,64,512]{2,1,0:T(8,128)(2,1)}), bf16[32,64,512]{2,1,0:T(8,128)(2,1)S(1)}, u32[]{:S(2)}, u32[]{:S(2)}) async-start(bf16[32,64,512]{2,1,0:T(8,128)(2,1)} %bitcast.2), calls=%async_computation | async-start | bytes 4194304 | tf_op jit(solution)/shard_map/all_to_all | solution.py:88
  178.7 0.7 dynamic-slice_bitcast_fusion
  179.4 0.8 multiply_reduce_fusion.3
  180.3 90.1 %all-reduce = (f32[]{:T(128)}, f32[]{:T(128)}) all-reduce(f32[]{:T(128)} %multiply_reduce_fusion.3, f32[]{:T(128)} %get-tuple-element.7), channel_id=1, replica_groups=mesh['dp'=32,'tensor'=8] {'dp','tensor'}, use_global_device_ids=true, to_apply=%region_1.2 | all-reduce | flops 2 | bytes 16 | tf_op jit(solution)/shard_map/psum | solution.py:60
  271.7 0.0 all-to-all-done
  271.7 1.2 fusion.11
  272.9 0.9 copy.12
  (9 shorter events, 0.1 us)
Async XLA Ops:
  7.2 134.3 %all-gather.2.cloned.1.call-start = ((), (), s32[]{:S(2)}) async-start(), calls=%async_computation.1 | async-start | bytes 15138816 | tf_op jit(solution)/shard_map/all_gather | solution.py:55
  144.6 16.8 %copy-start.2 = (f32[512,512]{1,0:T(8,128)}, f32[512,512]{1,0:T(8,128)S(1)}, u32[]{:S(2)}) copy-start(f32[512,512]{1,0:T(8,128)S(1)} %get-tuple-element.12) | copy-start | bytes 3145732
  147.3 4.8 %copy-start.1 = (f32[1,1,512,512]{3,2,1,0:T(8,128)S(1)}, f32[1,1,512,512]{3,2,1,0:T(8,128)}, u32[]{:S(2)}) copy-start(f32[1,1,512,512]{3,2,1,0:T(8,128)} %param.6) | copy-start | bytes 3145732
  154.9 9.5 %copy-start.3 = (f32[512,512]{1,0:T(8,128)}, f32[512,512]{1,0:T(8,128)S(1)}, u32[]{:S(2)}) copy-start(f32[512,512]{1,0:T(8,128)S(1)} %get-tuple-element.10) | copy-start | bytes 3145732
  157.7 3.7 %copy-start.5 = (f32[512,512]{1,0:T(8,128)S(1)}, f32[512,512]{1,0:T(8,128)}, u32[]{:S(2)}) copy-start(f32[512,512]{1,0:T(8,128)} %fusion.8) | copy-start | bytes 3145732
  164.4 2.0 copy-start.4
  169.0 10.4 %copy-start = (bf16[64,3584]{1,0:T(8,128)(2,1)S(1)}, bf16[64,3584]{1,0:T(8,128)(2,1)}, u32[]{:S(2)}) copy-start(bf16[64,3584]{1,0:T(8,128)(2,1)} %param.4) | copy-start | bytes 1376260
  171.0 100.7 %all-to-all-start = ((bf16[32,64,512]{2,1,0:T(8,128)(2,1)}), bf16[32,64,512]{2,1,0:T(8,128)(2,1)S(1)}, u32[]{:S(2)}, u32[]{:S(2)}) async-start(bf16[32,64,512]{2,1,0:T(8,128)(2,1)} %bitcast.2), calls=%async_computation | async-start | bytes 4194304 | tf_op jit(solution)/shard_map/all_to_all | solution.py:88
Sparse Core Ops, SparseCore 0:
  10.6 130.8 all-gather.1
where the time goes:
time: 283 us; the launch traced here: 281 us
  waiting for transfers between devices  130 us (46%)
  blocking collectives  90.1 us (32%)
  matrix products  27.2 us (10%)
  between operations  19.6 us (7%)
  starting transfers between devices  7.74 us (3%)
  other arithmetic  4.29 us (2%)
    all_gather x1, waiting for transfers between devices, body(): lax.all_gather(gradient, 'dp', axis=0, tiled=True)  129 us
    psum x1, blocking collectives, body(): grad_total = lax.psum(grad_local, ('dp', 'tensor'))  90.1 us
    dot_general x8, matrix products, matmul_full(): jnp.einsum('kab,kbc->kac', left, right, precision=lax.Precision.HIGHEST,...  17.3 us
    all_to_all x1, starting transfers between devices, body(): lax.all_to_all(back_rows.reshape(row_blocks * block_size, block_size), 'd...  7.7 us
  transfers between devices with their start and end apart: 2, of which 1 were waited for; matrix products, arithmetic and copies ran while one was open for 1% of the time, Pallas kernels for 0%

commit v1 on v0

v1 whole, which is shorter than its diff:
```python
import functools

import jax
import jax.numpy as jnp
from jax import lax
from jax.experimental import pallas as pl
from jax.experimental.pallas import tpu as pltpu
from jax.sharding import Mesh
from jax.sharding import PartitionSpec as P

DECAY = 0.9
EPSILON = 1e-06
NX = 4
NZ = 8
NT = 8
COLS = 7
BS = 512
VMEM_LIMIT = 48 * 1024 * 1024

T5 = [3.0517578125, -3.0517578125, 1.220703125, -0.244140625, 0.0244140625, -0.0009765625]
C0 = 25.0 / 16.0
C1 = -5.0 / 16.0 - T5[0] / 4.0
C2, C3, C4, C5, C6 = (-t / 4.0 for t in T5[1:])


def slot_of(owner):
    return (owner & (NZ - 1)) * NX + (owner >> 3)


def scatter_kernel(owner_ref, rows_ref, out_ref):
    out_ref[...] = jnp.zeros_like(out_ref)
    for i in range(NX):
        for j in range(COLS):
            out_ref[slot_of(owner_ref[i, j])] = rows_ref[i, :, j * BS : (j + 1) * BS]


def gather_kernel(owner_ref, scale_ref, slots_ref, out_ref):
    scale = scale_ref[0, 0]
    for i in range(NX):
        for j in range(COLS):
            piece = slots_ref[slot_of(owner_ref[i, j])].astype(jnp.float32)
            out_ref[i, :, j * BS : (j + 1) * BS] = (scale * piece).astype(jnp.bfloat16)


def dot(a, b):
    return jnp.dot(a, b, preferred_element_type=jnp.float32)


def dot_nt(a, b):
    return lax.dot_general(a, b, (((1,), (1,)), ((), ())), preferred_element_type=jnp.float32)


def dot_tn(a, b):
    return lax.dot_general(a, b, (((0,), (0,)), ((), ())), preferred_element_type=jnp.float32)


def split(x):
    high = x.astype(jnp.bfloat16)
    return high, (x - high.astype(jnp.float32)).astype(jnp.bfloat16)


def dot3(a, b):
    return dot(a[0], b[0]) + (dot(a[0], b[1]) + dot(a[1], b[0]))


def root(stats):
    frob = jnp.sqrt(jnp.sum(stats * stats, keepdims=True) + EPSILON)
    n = stats * (1.0 / frob)
    n_parts = split(n)
    x = dot3(n_parts, n_parts)
    x_parts = split(x)
    tail = C4 * x + dot(x_parts[0], (C5 * n + C6 * x).astype(jnp.bfloat16))
    y = dot3(x_parts, split(C3 * n + tail))
    row = lax.broadcasted_iota(jnp.int32, n.shape, 0)
    col = lax.broadcasted_iota(jnp.int32, n.shape, 1)
    total = jnp.where(row == col, C0, 0.0) + (C1 * n + C2 * x) + y
    return (total * lax.rsqrt(jnp.sqrt(frob))).astype(jnp.bfloat16)


def refresh_kernel(block_ref, left_ref, right_ref, packed_ref, left_out, right_out, sum_ref):
    block = block_ref[...]
    right = DECAY * right_ref[...] + ((1.0 - DECAY) / BS) * dot_tn(block, block)
    right_out[...] = right
    left = DECAY * left_ref[...] + ((1.0 - DECAY) / BS) * dot_nt(block, block)
    left_out[...] = left
    half = dot(block, root(right)).astype(jnp.bfloat16)
    conditioned = dot(root(left), half)
    packed_ref[...] = conditioned.astype(jnp.bfloat16)
    sum_ref[...] = jnp.broadcast_to(
        jnp.sum(conditioned * conditioned, keepdims=True), sum_ref.shape
    )


SMEM = functools.partial(pl.BlockSpec, memory_space=pltpu.SMEM)
VMEM = functools.partial(pl.BlockSpec, memory_space=pltpu.VMEM)
PARAMS = pltpu.CompilerParams(vmem_limit_bytes=VMEM_LIMIT)


def body(gradient, owner, prev_left, prev_right):
    rows, cols = gradient.shape
    part = rows // NX
    table = owner[0]
    f32, bf16 = jnp.float32, jnp.bfloat16

    spread = lax.all_to_all(gradient.reshape(NX, part, cols), "x", 0, 0, tiled=True)
    slots = pl.pallas_call(
        scatter_kernel,
        out_shape=jax.ShapeDtypeStruct((NX * NZ, part, BS), bf16),
        in_specs=[SMEM(), VMEM()],
        out_specs=VMEM(),
        compiler_params=PARAMS,
        name="scatter",
    )(table, spread)
    block = lax.all_to_all(slots, ("z", "x"), 0, 0, tiled=True).reshape(BS, BS)
    grad_local = jnp.sum(jnp.square(gradient.astype(f32)))

    packed, left, right, cond = pl.pallas_call(
        refresh_kernel,
        out_shape=[
            jax.ShapeDtypeStruct((BS, BS), bf16),
            jax.ShapeDtypeStruct((BS, BS), f32),
            jax.ShapeDtypeStruct((BS, BS), f32),
            jax.ShapeDtypeStruct((8, 128), f32),
        ],
        in_specs=[VMEM()] * 3,
        out_specs=[VMEM()] * 4,
        compiler_params=PARAMS,
        name="refresh",
    )(block, prev_left[0, 0], prev_right[0, 0])

    returned = lax.all_to_all(packed.reshape(NX * NZ, part, BS), ("z", "x"), 0, 0, tiled=True)
    both = jnp.stack([jnp.full((8, 128), grad_local, f32), cond])
    both = jnp.sum(
        lax.all_to_all(jnp.broadcast_to(both, (NX * NZ, 2, 8, 128)), ("z", "x"), 0, 0, tiled=True), 0
    )
    both = jnp.sum(
        lax.all_to_all(jnp.broadcast_to(both, (NT, 2, 8, 128)), ("y", "c"), 0, 0, tiled=True), 0
    )
    scale = jnp.sqrt(both[0, :1, :1] / (both[1, :1, :1] + EPSILON))
    update = pl.pallas_call(
        gather_kernel,
        out_shape=jax.ShapeDtypeStruct((NX, part, cols), bf16),
        in_specs=[SMEM(), SMEM(), VMEM()],
        out_specs=VMEM(),
        compiler_params=PARAMS,
        name="gather",
    )(table, scale, returned)
    update = lax.all_to_all(update, "x", 0, 0, tiled=True).reshape(rows, cols)
    return update, left[None, None], right[None, None]


def solution(mesh):
    wide = Mesh(mesh.devices.reshape(NX, NZ, NT // 2, 2), ("x", "z", "y", "c"))
    dp, tensor = ("x", "z"), ("y", "c")
    return jax.shard_map(
        body,
        mesh=wide,
        in_specs=(
            P(dp, tensor),
            P(tensor, None, None),
            P(tensor, dp, None, None),
            P(tensor, dp, None, None),
        ),
        out_specs=(P(dp, tensor), P(tensor, dp, None, None), P(tensor, dp, None, None)),
        check_vma=False,
    )
```

time: 283 us -> 109 us (0.39)
  waiting for transfers between devices: 130 us -> 30.5 us
  blocking collectives: 90.1 us -> 49.4 us
  matrix products: 27.2 us -> 0 us
  between operations: 19.6 us -> 2.05 us
  Pallas kernels: 0 us -> 8.98 us
  starting transfers between devices: 7.74 us -> 14.1 us
  other arithmetic: 4.29 us -> 0.88 us
    all_gather x1 -> x0, waiting for transfers between devices: 129 us -> none  [body(): lax.all_gather(gradient, 'dp', axis=0, tiled=True)]
    psum x1 -> x0, blocking collectives: 90.1 us -> none  [body(): grad_total = lax.psum(grad_local, ('dp', 'tensor'))]
    all_to_all x0 -> x4, blocking collectives: none -> 49.4 us  [the longest x1 15.7 us: body(): lax.all_to_all(jnp.broadcast_to(both, (NX * NZ, 2, 8, 128)), ('z', 'x'),...]
    all_to_all x1 -> x2, waiting for transfers between devices: 0.01 us -> 30.5 us  [the longest x1 15.5 us: body(): lax.all_to_all(packed.reshape(NX * NZ, part, BS), ('z', 'x'), 0, 0, tiled...]
    dot_general x12 -> x0, matrix products: 27.2 us -> none  [the longest x8 17.3 us: matmul_full(): jnp.einsum('kab,kbc->kac', left, right, precision=lax.Precision.HIGHEST,...]
    pallas_call x0 -> x3, Pallas kernels: none -> 8.98 us  [the longest x1 6.9 us: body(): pl.pallas_call(refresh_kernel, out_shape=[jax.ShapeDtypeStruct((BS, BS),...]
    all_to_all x1 -> x2, starting transfers between devices: 7.7 us -> 14.1 us  [the longest x1 9.33 us: body(): block = lax.all_to_all(slots, ('z', 'x'), 0, 0, tiled=True).reshape(BS, BS)]
  transfers between devices with their start and end apart: 2 -> 2, of which waited for: 1 -> 2; matrix products, arithmetic and copies ran while one was open for 1% -> 1% of each run, Pallas kernels for 0% -> 0%
where the time goes in v1:
time: 109 us; the launch traced here: 108 us
  blocking collectives  49.4 us (45%)
  waiting for transfers between devices  30.5 us (28%)
  starting transfers between devices  14.1 us (13%)
  Pallas kernels  8.98 us (8%)
  between operations  2.05 us (2%)
  local copies, waits for them, and re-layouts  2.04 us (2%)
    all_to_all x1, blocking collectives, body(): lax.all_to_all(jnp.broadcast_to(both, (NX * NZ, 2, 8, 128)), ('z', 'x'),...  15.7 us
    all_to_all x1, waiting for transfers between devices, body(): lax.all_to_all(packed.reshape(NX * NZ, part, BS), ('z', 'x'), 0, 0, tiled...  15.5 us
    all_to_all x1, waiting for transfers between devices, body(): block = lax.all_to_all(slots, ('z', 'x'), 0, 0, tiled=True).reshape(BS, BS)  14.9 us
    all_to_all x1, blocking collectives, body(): lax.all_to_all(gradient.reshape(NX, part, cols), 'x', 0, 0, tiled=True)  13.2 us
    all_to_all x1, blocking collectives, body(): update = lax.all_to_all(update, 'x', 0, 0, tiled=True).reshape(rows, cols)  10.6 us
    all_to_all x1, blocking collectives, body(): lax.all_to_all(jnp.broadcast_to(both, (NT, 2, 8, 128)), ('y', 'c'), 0, 0,...  9.89 us
    all_to_all x1, starting transfers between devices, body(): block = lax.all_to_all(slots, ('z', 'x'), 0, 0, tiled=True).reshape(BS, BS)  9.33 us
    pallas_call x1, Pallas kernels, body(): pl.pallas_call(refresh_kernel, out_shape=[jax.ShapeDtypeStruct((BS, BS),...  6.9 us
  transfers between devices with their start and end apart: 2, of which 2 were waited for; matrix products, arithmetic and copies ran while one was open for 1% of the time, Pallas kernels for 0%

profile of v1, /device:TPU:32, one launch (start us, length us, event | category | flops | bytes accessed | tf_op | source)
XLA Modules:
  0.0 107.9 jit_solution(3783297086080113415)
XLA Ops:
  0.6 0.0 copy-start.2
  0.6 0.0 copy-start.3
  0.6 13.2 %all_to_all.30.rows_ref = bf16[4,16,3584]{2,1,0:T(8,128)(2,1)S(1)} all-to-all(bf16[4,16,3584]{2,1,0:T(8,128)(2,1)} %bitcast.18), channel_id=1, replica_groups=mesh['x'=4,'z'=8,'y'=4,'c'=2] {'x'}, dimensions={0} | all-to-all | bytes 917504 | tf_op jit(solution)/shard_map/all_to_all | solution.py:105
  13.9 0.0 copy-done.2
  13.9 0.0 copy-start
  13.9 0.0 copy-start.1
  13.9 1.4 %scatter.1 = bf16[32,16,512]{2,1,0:T(8,128)(2,1)} custom-call(s32[4,7]{1,0:T(4,128)S(1)} %bitcast.14, bf16[4,16,3584]{2,1,0:T(8,128)(2,1)S(1)} %all_to_all.30.rows_ref), custom_call_target="tpu_custom_call" | custom-call | tf_op jit(solution)/shard_map/scatter/pallas_call | solution.py:106
  15.3 9.3 %all-to-all-start.1 = ((bf16[32,16,512]{2,1,0:T(8,128)(2,1)}), bf16[32,16,512]{2,1,0:T(8,128)(2,1)S(1)}, u32[]{:S(2)}, u32[]{:S(2)}) async-start(bf16[32,16,512]{2,1,0:T(8,128)(2,1)} %scatter.1), calls=%async_computation.1 | async-start | bytes 1048576 | tf_op jit(solution)/shard_map/all_to_all | solution.py:114
  24.6 0.0 copy-done.3
  24.7 0.8 multiply_reduce_fusion
  25.5 14.9 %all-to-all-done.1 = bf16[32,16,512]{2,1,0:T(8,128)(2,1)S(1)} async-done(((bf16[32,16,512]{2,1,0:T(8,128)(2,1)}), bf16[32,16,512]{2,1,0:T(8,128)(2,1)S(1)}, u32[]{:S(2)}, u32[]{:S(2)}) %all-to-all-start.1) | async-done | bytes 524320 | tf_op jit(solution)/shard_map/all_to_all | solution.py:114
  40.4 0.0 copy-done
  40.4 0.0 copy-done.1
  40.4 6.9 %refresh.1 = (bf16[512,512]{1,0:T(8,128)(2,1)}, f32[512,512]{1,0:T(8,128)}, f32[512,512]{1,0:T(8,128)}, f32[8,128]{1,0:T(8,128)S(1)}) custom-call(bf16[512,512]{1,0:T(8,128)(2,1)S(1)} %bitcast.11, f32[512,512]{1,0:T(8,128)S(1)} %bitcast.12, f32[512,512]{1,0:T(8,128)S(1)} %bitcast.13), custom_call_target="tpu_custom_call" | custom-call | tf_op jit(solution)/shard_map/refresh/pallas_call | solution.py:117
  47.3 0.6 stack.7
  48.0 15.7 %all_to_all.31 = f32[32,2,8,128]{3,2,1,0:T(8,128)S(1)} all-to-all(f32[32,2,8,128]{3,2,1,0:T(8,128)S(1)} %broadcast_in_dim.12), channel_id=1, replica_groups=mesh['x'=4,'z'=8,'y'=4,'c'=2] {'z','x'}, dimensions={0} | all-to-all | bytes 524288 | tf_op jit(solution)/shard_map/all_to_all | solution.py:134
  63.7 9.9 %all_to_all.32 = f32[8,2,8,128]{3,2,1,0:T(8,128)S(1)} all-to-all(f32[8,2,8,128]{3,2,1,0:T(8,128)S(1)} %broadcast_in_dim.13), channel_id=1, replica_groups=mesh['x'=4,'z'=8,'y'=4,'c'=2] {'y','c'}, dimensions={0} | all-to-all | bytes 131072 | tf_op jit(solution)/shard_map/all_to_all | solution.py:137
  73.6 4.7 %all-to-all-start.4 = ((bf16[32,16,512]{2,1,0:T(8,128)(2,1)}), bf16[32,16,512]{2,1,0:T(8,128)(2,1)S(1)}, u32[]{:S(2)}, u32[]{:S(2)}) async-start(bf16[32,16,512]{2,1,0:T(8,128)(2,1)} %bitcast.7), calls=%async_computation.4 | async-start | bytes 1048576 | tf_op jit(solution)/shard_map/all_to_all | solution.py:131
  78.4 0.6 fusion
  80.3 15.5 %all-to-all-done.4.slots_ref = bf16[32,16,512]{2,1,0:T(8,128)(2,1)S(1)} async-done(((bf16[32,16,512]{2,1,0:T(8,128)(2,1)}), bf16[32,16,512]{2,1,0:T(8,128)(2,1)S(1)}, u32[]{:S(2)}, u32[]{:S(2)}) %all-to-all-start.4) | async-done | bytes 524320 | tf_op jit(solution)/shard_map/all_to_all | solution.py:131
  95.8 0.6 gather.1
  96.5 10.6 %all_to_all.33 = bf16[4,16,3584]{2,1,0:T(8,128)(2,1)S(1)} all-to-all(bf16[4,16,3584]{2,1,0:T(8,128)(2,1)S(1)} %gather.1), channel_id=1, replica_groups=mesh['x'=4,'z'=8,'y'=4,'c'=2] {'x'}, dimensions={0} | all-to-all | bytes 917504 | tf_op jit(solution)/shard_map/all_to_all | solution.py:148
  107.1 0.8 copy.8
  (4 shorter events, 0.1 us)
Async XLA Ops:
  0.6 13.2 %copy-start.2 = (s32[1,4,7]{2,1,0:T(4,128)S(1)}, s32[1,4,7]{2,1,0:T(4,128)}, u32[]{:S(2)}) copy-start(s32[1,4,7]{2,1,0:T(4,128)} %param.5) | copy-start | bytes 340
  0.6 24.0 %copy-start.3 = (bf16[64,3584]{1,0:T(8,128)(2,1)S(1)}, bf16[64,3584]{1,0:T(8,128)(2,1)}, u32[]{:S(2)}) copy-start(bf16[64,3584]{1,0:T(8,128)(2,1)} %param.4) | copy-start | bytes 1376260
  13.9 26.6 %copy-start = (f32[1,1,512,512]{3,2,1,0:T(8,128)S(1)}, f32[1,1,512,512]{3,2,1,0:T(8,128)}, u32[]{:S(2)}) copy-start(f32[1,1,512,512]{3,2,1,0:T(8,128)} %param.6) | copy-start | bytes 3145732
  13.9 26.6 %copy-start.1 = (f32[1,1,512,512]{3,2,1,0:T(8,128)S(1)}, f32[1,1,512,512]{3,2,1,0:T(8,128)}, u32[]{:S(2)}) copy-start(f32[1,1,512,512]{3,2,1,0:T(8,128)} %param.7) | copy-start | bytes 3145732
  15.3 25.1 %all-to-all-start.1 = ((bf16[32,16,512]{2,1,0:T(8,128)(2,1)}), bf16[32,16,512]{2,1,0:T(8,128)(2,1)S(1)}, u32[]{:S(2)}, u32[]{:S(2)}) async-start(bf16[32,16,512]{2,1,0:T(8,128)(2,1)} %scatter.1), calls=%async_computation.1 | async-start | bytes 1048576 | tf_op jit(solution)/shard_map/all_to_all | solution.py:114
  73.6 22.2 %all-to-all-start.4 = ((bf16[32,16,512]{2,1,0:T(8,128)(2,1)}), bf16[32,16,512]{2,1,0:T(8,128)(2,1)S(1)}, u32[]{:S(2)}, u32[]{:S(2)}) async-start(bf16[32,16,512]{2,1,0:T(8,128)(2,1)} %bitcast.7), calls=%async_computation.4 | async-start | bytes 1048576 | tf_op jit(solution)/shard_map/all_to_all | solution.py:131

commit v2 on v1

--- a/solution.py
+++ b/solution.py
@@ -15,6 +15,10 @@
 NT = 8
 COLS = 7
 BS = 512
+LANES = 128
+TILES = BS // LANES
+PART = 16
+EXTRA = 8
 VMEM_LIMIT = 48 * 1024 * 1024
 
 T5 = [3.0517578125, -3.0517578125, 1.220703125, -0.244140625, 0.0244140625, -0.0009765625]
@@ -34,12 +38,24 @@
             out_ref[slot_of(owner_ref[i, j])] = rows_ref[i, :, j * BS : (j + 1) * BS]
 
 
-def gather_kernel(owner_ref, scale_ref, slots_ref, out_ref):
-    scale = scale_ref[0, 0]
+def gather_kernel(owner_ref, slots_ref, out_ref, sums_ref):
     for i in range(NX):
         for j in range(COLS):
-            piece = slots_ref[slot_of(owner_ref[i, j])].astype(jnp.float32)
-            out_ref[i, :, j * BS : (j + 1) * BS] = (scale * piece).astype(jnp.bfloat16)
+            slot = slot_of(owner_ref[i, j])
+            for t in range(TILES):
+                out_ref[i, :, j * BS + t * LANES : j * BS + (t + 1) * LANES] = slots_ref[
+                    slot, t * PART : (t + 1) * PART, :
+                ]
+    lines = jnp.sum(slots_ref[:, TILES * PART :, :].astype(jnp.float32), axis=0)
+    grad = lines[0:1] + (lines[1:2] + lines[2:3])
+    cond = lines[3:4] + (lines[4:5] + lines[5:6])
+    line = lax.broadcasted_iota(jnp.int32, sums_ref.shape, 0)
+    sums_ref[...] = jnp.where(line < 4, grad, cond)
+
+
+def finish_kernel(sums_ref, rows_ref, out_ref):
+    scale = jnp.sqrt(sums_ref[0:1, 0:1] / (sums_ref[4:5, 0:1] + EPSILON))
+    out_ref[...] = (scale * rows_ref[...].astype(jnp.float32)).astype(jnp.bfloat16)
 
 
 def dot(a, b):
@@ -77,7 +93,9 @@
     return (total * lax.rsqrt(jnp.sqrt(frob))).astype(jnp.bfloat16)
 
 
-def refresh_kernel(block_ref, left_ref, right_ref, packed_ref, left_out, right_out, sum_ref):
+def refresh_kernel(
+    grad_ref, block_ref, left_ref, right_ref, packed_ref, left_out, right_out
+):
     block = block_ref[...]
     right = DECAY * right_ref[...] + ((1.0 - DECAY) / BS) * dot_tn(block, block)
     right_out[...] = right
@@ -85,15 +103,31 @@
     left_out[...] = left
     half = dot(block, root(right)).astype(jnp.bfloat16)
     conditioned = dot(root(left), half)
-    packed_ref[...] = conditioned.astype(jnp.bfloat16)
-    sum_ref[...] = jnp.broadcast_to(
-        jnp.sum(conditioned * conditioned, keepdims=True), sum_ref.shape
-    )
+    packed = conditioned.astype(jnp.bfloat16)
+    for t in range(TILES):
+        packed_ref[:, t * PART : (t + 1) * PART, :] = packed[
+            :, t * LANES : (t + 1) * LANES
+        ].reshape(NX * NZ, PART, LANES)
+    line = lax.broadcasted_iota(jnp.int32, (EXTRA, LANES), 0)
+    rest = jnp.where(line < 3, grad_ref[0, 0], jnp.sum(conditioned * conditioned, keepdims=True))
+    high = rest.astype(jnp.bfloat16).astype(jnp.float32)
+    rest = rest - high
+    middle = rest.astype(jnp.bfloat16).astype(jnp.float32)
+    low = rest - middle
+    kind = jnp.where(line < 3, line, line - 3)
+    terms = jnp.where(kind == 0, high, jnp.where(kind == 1, middle, low)).astype(jnp.bfloat16)
+    packed_ref[:, TILES * PART :, :] = jnp.broadcast_to(terms[None], (NX * NZ, EXTRA, LANES))
 
 
 SMEM = functools.partial(pl.BlockSpec, memory_space=pltpu.SMEM)
 VMEM = functools.partial(pl.BlockSpec, memory_space=pltpu.VMEM)
 PARAMS = pltpu.CompilerParams(vmem_limit_bytes=VMEM_LIMIT)
+
+
+def total(value):
+    for axis, partner in (("c", (1, 0)), ("y", (1, 0, 3, 2)), ("y", (3, 2, 1, 0))):
+        value = value + lax.ppermute(value, axis, list(enumerate(partner)))
+    return value
 
 
 def body(gradient, owner, prev_left, prev_right):
@@ -114,38 +148,40 @@
     block = lax.all_to_all(slots, ("z", "x"), 0, 0, tiled=True).reshape(BS, BS)
     grad_local = jnp.sum(jnp.square(gradient.astype(f32)))
 
-    packed, left, right, cond = pl.pallas_call(
+    packed, left, right = pl.pallas_call(
         refresh_kernel,
         out_shape=[
-            jax.ShapeDtypeStruct((BS, BS), bf16),
+            jax.ShapeDtypeStruct((NX * NZ, TILES * PART + EXTRA, LANES), bf16),
             jax.ShapeDtypeStruct((BS, BS), f32),
             jax.ShapeDtypeStruct((BS, BS), f32),
-            jax.ShapeDtypeStruct((8, 128), f32),
         ],
-        in_specs=[VMEM()] * 3,
-        out_specs=[VMEM()] * 4,
+        in_specs=[SMEM()] + [VMEM()] * 3,
+        out_specs=[VMEM()] * 3,
         compiler_params=PARAMS,
         name="refresh",
-    )(block, prev_left[0, 0], prev_right[0, 0])
-
-    returned = lax.all_to_all(packed.reshape(NX * NZ, part, BS), ("z", "x"), 0, 0, tiled=True)
-    both = jnp.stack([jnp.full((8, 128), grad_local, f32), cond])
-    both = jnp.sum(
-        lax.all_to_all(jnp.broadcast_to(both, (NX * NZ, 2, 8, 128)), ("z", "x"), 0, 0, tiled=True), 0
-    )
-    both = jnp.sum(
-        lax.all_to_all(jnp.broadcast_to(both, (NT, 2, 8, 128)), ("y", "c"), 0, 0, tiled=True), 0
-    )
-    scale = jnp.sqrt(both[0, :1, :1] / (both[1, :1, :1] + EPSILON))
+    )(grad_local.reshape(1, 1), block, prev_left[0, 0], prev_right[0, 0])
+
+    returned = lax.all_to_all(packed, ("z", "x"), 0, 0, tiled=True)
+    update, sums = pl.pallas_call(
+        gather_kernel,
+        out_shape=[
+            jax.ShapeDtypeStruct((NX, part, cols), bf16),
+            jax.ShapeDtypeStruct((8, LANES), f32),
+        ],
+        in_specs=[SMEM(), VMEM()],
+        out_specs=[VMEM()] * 2,
+        compiler_params=PARAMS,
+        name="gather",
+    )(table, returned)
+    update = lax.all_to_all(update, "x", 0, 0, tiled=True).reshape(rows, cols)
     update = pl.pallas_call(
-        gather_kernel,
-        out_shape=jax.ShapeDtypeStruct((NX, part, cols), bf16),
-        in_specs=[SMEM(), SMEM(), VMEM()],
+        finish_kernel,
+        out_shape=jax.ShapeDtypeStruct((rows, cols), bf16),
+        in_specs=[VMEM()] * 2,
         out_specs=VMEM(),
         compiler_params=PARAMS,
-        name="gather",
-    )(table, scale, returned)
-    update = lax.all_to_all(update, "x", 0, 0, tiled=True).reshape(rows, cols)
+        name="finish",
+    )(total(sums), update)
     return update, left[None, None], right[None, None]
 
 

time: 109 us -> 86.5 us (0.79)
  blocking collectives: 49.4 us -> 35 us
  waiting for transfers between devices: 30.5 us -> 19.9 us
  starting transfers between devices: 14.1 us -> 17.5 us
  local copies, waits for them, and re-layouts: 2.04 us -> 0.02 us
  Pallas kernels: 8.98 us -> 10.8 us
  between operations: 2.05 us -> 0.69 us
    all_to_all x1, waiting for transfers between devices: 15.5 us -> 0.01 us  [body(): update = lax.all_to_all(update, 'x', 0, 0, tiled=True).reshape(rows, cols)]
    all_to_all x3 -> x1, blocking collectives: 36.2 us -> 21.8 us  [body(): returned = lax.all_to_all(packed, ('z', 'x'), 0, 0, tiled=True)]
    ppermute x0 -> x3, waiting for transfers between devices: none -> 4.97 us  [total(): value = value + lax.ppermute(value, axis, list(enumerate(partner)))]
    ppermute x0 -> x3, starting transfers between devices: none -> 4.7 us  [total(): value = value + lax.ppermute(value, axis, list(enumerate(partner)))]
    pallas_call x2 -> x3, Pallas kernels: 7.55 us -> 9.36 us  [the longest x1 6.97 us: body(): pl.pallas_call(refresh_kernel, out_shape=[jax.ShapeDtypeStruct((NX * NZ,...]
    all_to_all x1, starting transfers between devices: 4.75 us -> 3.47 us  [body(): update = lax.all_to_all(update, 'x', 0, 0, tiled=True).reshape(rows, cols)]
  transfers between devices with their start and end apart: 2 -> 5, of which waited for: 2 -> 4; matrix products, arithmetic and copies ran while one was open for 1% -> 1% of each run, Pallas kernels for 0% -> 0%
where the time goes in v2:
time: 86.5 us; the launch traced here: 84.8 us
  blocking collectives  35 us (40%)
  waiting for transfers between devices  19.9 us (23%)
  starting transfers between devices  17.5 us (20%)
  Pallas kernels  10.8 us (12%)
    all_to_all x1, blocking collectives, body(): returned = lax.all_to_all(packed, ('z', 'x'), 0, 0, tiled=True)  21.8 us
    all_to_all x1, waiting for transfers between devices, body(): block = lax.all_to_all(slots, ('z', 'x'), 0, 0, tiled=True).reshape(BS, BS)  14.9 us
    all_to_all x1, blocking collectives, body(): lax.all_to_all(gradient.reshape(NX, part, cols), 'x', 0, 0, tiled=True)  13.2 us
    all_to_all x1, starting transfers between devices, body(): block = lax.all_to_all(slots, ('z', 'x'), 0, 0, tiled=True).reshape(BS, BS)  9.33 us
    pallas_call x1, Pallas kernels, body(): pl.pallas_call(refresh_kernel, out_shape=[jax.ShapeDtypeStruct((NX * NZ,...  6.97 us
    ppermute x3, waiting for transfers between devices, total(): value = value + lax.ppermute(value, axis, list(enumerate(partner)))  4.97 us
    ppermute x3, starting transfers between devices, total(): value = value + lax.ppermute(value, axis, list(enumerate(partner)))  4.7 us
    all_to_all x1, starting transfers between devices, body(): update = lax.all_to_all(update, 'x', 0, 0, tiled=True).reshape(rows, cols)  3.47 us
  transfers between devices with their start and end apart: 5, of which 4 were waited for; matrix products, arithmetic and copies ran while one was open for 1% of the time, Pallas kernels for 0%

profile of v2, /device:TPU:32, one launch (start us, length us, event | category | flops | bytes accessed | tf_op | source)
XLA Modules:
  0.0 84.8 jit_solution(18200990685592337967)
XLA Ops:
  0.6 0.0 copy-start.2
  0.6 0.0 copy-start.3
  0.6 13.2 %all_to_all.20.rows_ref = bf16[4,16,3584]{2,1,0:T(8,128)(2,1)S(1)} all-to-all(bf16[4,16,3584]{2,1,0:T(8,128)(2,1)} %bitcast.15), channel_id=1, replica_groups=mesh['x'=4,'z'=8,'y'=4,'c'=2] {'x'}, dimensions={0} | all-to-all | bytes 917504 | tf_op jit(solution)/shard_map/all_to_all | solution.py:139
  13.9 0.0 copy-done.2
  13.9 0.0 copy-start
  13.9 0.0 copy-start.1
  13.9 1.4 %scatter.1 = bf16[32,16,512]{2,1,0:T(8,128)(2,1)} custom-call(s32[4,7]{1,0:T(4,128)S(1)} %bitcast.13, bf16[4,16,3584]{2,1,0:T(8,128)(2,1)S(1)} %all_to_all.20.rows_ref), custom_call_target="tpu_custom_call" | custom-call | tf_op jit(solution)/shard_map/scatter/pallas_call | solution.py:140
  15.3 9.3 %all-to-all-start.1 = ((bf16[32,16,512]{2,1,0:T(8,128)(2,1)}), bf16[32,16,512]{2,1,0:T(8,128)(2,1)S(1)}, u32[]{:S(2)}, u32[]{:S(2)}) async-start(bf16[32,16,512]{2,1,0:T(8,128)(2,1)} %scatter.1), calls=%async_computation.1 | async-start | bytes 1048576 | tf_op jit(solution)/shard_map/all_to_all | solution.py:148
  24.6 0.0 copy-done.3
  24.7 0.8 multiply_reduce_fusion
  25.5 14.9 %all-to-all-done.1 = bf16[32,16,512]{2,1,0:T(8,128)(2,1)S(1)} async-done(((bf16[32,16,512]{2,1,0:T(8,128)(2,1)}), bf16[32,16,512]{2,1,0:T(8,128)(2,1)S(1)}, u32[]{:S(2)}, u32[]{:S(2)}) %all-to-all-start.1) | async-done | bytes 524320 | tf_op jit(solution)/shard_map/all_to_all | solution.py:148
  40.4 0.0 copy-done
  40.4 0.0 copy-done.1
  40.4 7.0 %refresh.1 = (bf16[32,72,128]{2,1,0:T(8,128)(2,1)S(1)}, f32[512,512]{1,0:T(8,128)}, f32[512,512]{1,0:T(8,128)}) custom-call(f32[1,1]{1,0:T(1,128)} %bitcast.1.grad_ref, bf16[512,512]{1,0:T(8,128)(2,1)S(1)} %bitcast.9, f32[512,512]{1,0:T(8,128)S(1)} %bitcast.11, f32[512,512]{1,0:T(8,128)S(1)} %bitcast.12), custom_call_target="tpu_custom_call" | custom-call | tf_op jit(solution)/shard_map/refresh/pallas_call | solution.py:151
  47.4 21.8 %all_to_all.21.slots_ref = bf16[32,72,128]{2,1,0:T(8,128)(2,1)S(1)} all-to-all(bf16[32,72,128]{2,1,0:T(8,128)(2,1)S(1)} %get-tuple-element.8), channel_id=1, replica_groups=mesh['x'=4,'z'=8,'y'=4,'c'=2] {'z','x'}, dimensions={0} | all-to-all | bytes 1179648 | tf_op jit(solution)/shard_map/all_to_all | solution.py:164
  69.2 1.4 %gather.1 = (bf16[4,16,3584]{2,1,0:T(8,128)(2,1)}, f32[8,128]{1,0:T(8,128)S(1)}) custom-call(s32[4,7]{1,0:T(4,128)S(1)} %bitcast.14, bf16[32,72,128]{2,1,0:T(8,128)(2,1)S(1)} %all_to_all.21.slots_ref), custom_call_target="tpu_custom_call" | custom-call | tf_op jit(solution)/shard_map/gather/pallas_call | solution.py:165
  70.7 3.5 %all-to-all-start.3 = ((bf16[4,16,3584]{2,1,0:T(8,128)(2,1)}), bf16[4,16,3584]{2,1,0:T(8,128)(2,1)S(1)}, u32[]{:S(2)}, u32[]{:S(2)}) async-start(bf16[4,16,3584]{2,1,0:T(8,128)(2,1)} %get-tuple-element.10), calls=%async_computation.3 | async-start | bytes 917504 | tf_op jit(solution)/shard_map/all_to_all | solution.py:176
  74.2 0.1 collective-permute-start
  74.3 1.2 %collective-permute-done = f32[8,128]{1,0:T(8,128)S(1)} collective-permute-done((f32[8,128]{1,0:T(8,128)S(1)}, f32[8,128]{1,0:T(8,128)S(1)}, u32[]{:S(2)}, u32[]{:S(2)}) %collective-permute-start) | collective-permute-done | bytes 4128 | tf_op jit(solution)/shard_map/ppermute | solution.py:129
  75.4 1.6 %collective-permute-start.1 = (f32[8,128]{1,0:T(8,128)S(1)}, f32[8,128]{1,0:T(8,128)S(1)}, u32[]{:S(2)}, u32[]{:S(2)}) collective-permute-start(f32[8,128]{1,0:T(8,128)S(1)} %add.9), channel_id=1, source_target_pairs={{0,2},{2,0},{4,6},{6,4},{1,3},{3,1},{5,7},{7,5},{8,10},{10,8},{12,... | collective-permute-start | bytes 12296 | tf_op jit(solution)/shard_map/ppermute | solution.py:129
  77.0 2.0 %collective-permute-done.1 = f32[8,128]{1,0:T(8,128)S(1)} collective-permute-done((f32[8,128]{1,0:T(8,128)S(1)}, f32[8,128]{1,0:T(8,128)S(1)}, u32[]{:S(2)}, u32[]{:S(2)}) %collective-permute-start.1) | collective-permute-done | bytes 4128 | tf_op jit(solution)/shard_map/ppermute | solution.py:129
  79.0 3.0 %collective-permute-start.2 = (f32[8,128]{1,0:T(8,128)S(1)}, f32[8,128]{1,0:T(8,128)S(1)}, u32[]{:S(2)}, u32[]{:S(2)}) collective-permute-start(f32[8,128]{1,0:T(8,128)S(1)} %add.10), channel_id=1, source_target_pairs={{0,6},{2,4},{4,2},{6,0},{1,7},{3,5},{5,3},{7,1},{8,14},{10,12},{12... | collective-permute-start | bytes 12296 | tf_op jit(solution)/shard_map/ppermute | solution.py:129
  82.1 1.8 %collective-permute-done.2 = f32[8,128]{1,0:T(8,128)S(1)} collective-permute-done((f32[8,128]{1,0:T(8,128)S(1)}, f32[8,128]{1,0:T(8,128)S(1)}, u32[]{:S(2)}, u32[]{:S(2)}) %collective-permute-start.2) | collective-permute-done | bytes 4128 | tf_op jit(solution)/shard_map/ppermute | solution.py:129
  83.9 0.0 all-to-all-done.3
  83.9 0.9 %finish.1 = bf16[64,3584]{1,0:T(8,128)(2,1)} custom-call(f32[8,128]{1,0:T(8,128)S(1)} %add.11.sums_ref, bf16[64,3584]{1,0:T(8,128)(2,1)S(1)} %bitcast.10), custom_call_target="tpu_custom_call" | custom-call | tf_op jit(solution)/shard_map/finish/pallas_call | solution.py:177
  (3 shorter events, 0.0 us)
Async XLA Ops:
  0.6 13.2 %copy-start.2 = (s32[1,4,7]{2,1,0:T(4,128)S(1)}, s32[1,4,7]{2,1,0:T(4,128)}, u32[]{:S(2)}) copy-start(s32[1,4,7]{2,1,0:T(4,128)} %param.5) | copy-start | bytes 340
  0.6 24.0 %copy-start.3 = (bf16[64,3584]{1,0:T(8,128)(2,1)S(1)}, bf16[64,3584]{1,0:T(8,128)(2,1)}, u32[]{:S(2)}) copy-start(bf16[64,3584]{1,0:T(8,128)(2,1)} %param.4) | copy-start | bytes 1376260
  13.9 26.6 %copy-start = (f32[1,1,512,512]{3,2,1,0:T(8,128)S(1)}, f32[1,1,512,512]{3,2,1,0:T(8,128)}, u32[]{:S(2)}) copy-start(f32[1,1,512,512]{3,2,1,0:T(8,128)} %param.6) | copy-start | bytes 3145732
  13.9 26.6 %copy-start.1 = (f32[1,1,512,512]{3,2,1,0:T(8,128)S(1)}, f32[1,1,512,512]{3,2,1,0:T(8,128)}, u32[]{:S(2)}) copy-start(f32[1,1,512,512]{3,2,1,0:T(8,128)} %param.7) | copy-start | bytes 3145732
  15.3 25.1 %all-to-all-start.1 = ((bf16[32,16,512]{2,1,0:T(8,128)(2,1)}), bf16[32,16,512]{2,1,0:T(8,128)(2,1)S(1)}, u32[]{:S(2)}, u32[]{:S(2)}) async-start(bf16[32,16,512]{2,1,0:T(8,128)(2,1)} %scatter.1), calls=%async_computation.1 | async-start | bytes 1048576 | tf_op jit(solution)/shard_map/all_to_all | solution.py:148
  70.7 13.2 %all-to-all-start.3 = ((bf16[4,16,3584]{2,1,0:T(8,128)(2,1)}), bf16[4,16,3584]{2,1,0:T(8,128)(2,1)S(1)}, u32[]{:S(2)}, u32[]{:S(2)}) async-start(bf16[4,16,3584]{2,1,0:T(8,128)(2,1)} %get-tuple-element.10), calls=%async_computation.3 | async-start | bytes 917504 | tf_op jit(solution)/shard_map/all_to_all | solution.py:176
  74.2 1.3 %collective-permute-start = (f32[8,128]{1,0:T(8,128)S(1)}, f32[8,128]{1,0:T(8,128)S(1)}, u32[]{:S(2)}, u32[]{:S(2)}) collective-permute-start(f32[8,128]{1,0:T(8,128)S(1)} %get-tuple-element.9), channel_id=1, source_target_pairs={{0,1},{1,0},{2,3},{3,2},{4,5},{5,4},{6,7},{7,6},{8,9},{9,8},{10,11... | collective-permute-start | bytes 12296 | tf_op jit(solution)/shard_map/ppermute | solution.py:129
  75.4 3.6 %collective-permute-start.1 = (f32[8,128]{1,0:T(8,128)S(1)}, f32[8,128]{1,0:T(8,128)S(1)}, u32[]{:S(2)}, u32[]{:S(2)}) collective-permute-start(f32[8,128]{1,0:T(8,128)S(1)} %add.9), channel_id=1, source_target_pairs={{0,2},{2,0},{4,6},{6,4},{1,3},{3,1},{5,7},{7,5},{8,10},{10,8},{12,... | collective-permute-start | bytes 12296 | tf_op jit(solution)/shard_map/ppermute | solution.py:129
  79.0 4.8 %collective-permute-start.2 = (f32[8,128]{1,0:T(8,128)S(1)}, f32[8,128]{1,0:T(8,128)S(1)}, u32[]{:S(2)}, u32[]{:S(2)}) collective-permute-start(f32[8,128]{1,0:T(8,128)S(1)} %add.10), channel_id=1, source_target_pairs={{0,6},{2,4},{4,2},{6,0},{1,7},{3,5},{5,3},{7,1},{8,14},{10,12},{12... | collective-permute-start | bytes 12296 | tf_op jit(solution)/shard_map/ppermute | solution.py:129

commit v3 on v2

v3 whole, which is shorter than its diff:
```python
import functools

import jax
import jax.numpy as jnp
from jax import lax
from jax.experimental import pallas as pl
from jax.experimental.pallas import tpu as pltpu
from jax.sharding import Mesh
from jax.sharding import PartitionSpec as P

DECAY = 0.9
EPSILON = 1e-06
NX = 4
NZ = 8
NT = 8
COLS = 7
BS = 512
LANES = 128
TILES = BS // LANES
PART = 16
EXTRA = 8
VMEM_LIMIT = 48 * 1024 * 1024

T5 = [3.0517578125, -3.0517578125, 1.220703125, -0.244140625, 0.0244140625, -0.0009765625]
C0 = 25.0 / 16.0
C1 = -5.0 / 16.0 - T5[0] / 4.0
C2, C3, C4, C5, C6 = (-t / 4.0 for t in T5[1:])


def scatter_kernel(owner_ref, rows_ref, out_ref):
    out_ref[...] = jnp.zeros_like(out_ref)
    for i in range(NX):
        for j in range(COLS):
            out_ref[owner_ref[i, j]] = rows_ref[i, :, j * BS : (j + 1) * BS]


def sums_kernel(slots_ref, sums_ref):
    lines = jnp.sum(slots_ref[:, TILES * PART :, :].astype(jnp.float32), axis=0)
    grad = lines[0:1] + (lines[1:2] + lines[2:3])
    cond = lines[3:4] + (lines[4:5] + lines[5:6])
    line = lax.broadcasted_iota(jnp.int32, sums_ref.shape, 0)
    sums_ref[...] = jnp.where(line < 4, grad, cond)


def gather_kernel(owner_ref, after_ref, slots_ref, *out_refs):
    del after_ref
    for k, out_ref in enumerate(out_refs):
        for j in range(COLS):
            slot = owner_ref[NX + k, j]
            for t in range(TILES):
                out_ref[:, j * BS + t * LANES : j * BS + (t + 1) * LANES] = slots_ref[
                    slot, t * PART : (t + 1) * PART, :
                ]


def finish_kernel(x_ref, sums_ref, *refs):
    scale = jnp.sqrt(sums_ref[0:1, 0:1] / (sums_ref[4:5, 0:1] + EPSILON))
    out_ref = refs[NX]
    for k in range(NX):
        start = pl.multiple_of(((x_ref[0, 0] + NX - k) & (NX - 1)) * PART, PART)
        out_ref[pl.ds(start, PART), :] = (scale * refs[k][...].astype(jnp.float32)).astype(
            jnp.bfloat16
        )


def dot(a, b):
    return jnp.dot(a, b, preferred_element_type=jnp.float32)


def dot_nt(a, b):
    return lax.dot_general(a, b, (((1,), (1,)), ((), ())), preferred_element_type=jnp.float32)


def dot_tn(a, b):
    return lax.dot_general(a, b, (((0,), (0,)), ((), ())), preferred_element_type=jnp.float32)


def split(x):
    high = x.astype(jnp.bfloat16)
    return high, (x - high.astype(jnp.float32)).astype(jnp.bfloat16)


def normalize(stats):
    frob = jnp.sqrt(jnp.sum(stats * stats, keepdims=True) + EPSILON)
    return frob, stats * (1.0 / frob)


def square(n):
    high = n.astype(jnp.bfloat16)
    low2 = (2.0 * (n - high.astype(jnp.float32))).astype(jnp.bfloat16)
    return high, dot(high, high) + dot(high, low2)


def upper_terms(n, n_high, x):
    x_high = x.astype(jnp.bfloat16)
    mixed = n_high * jnp.bfloat16(C5) + x_high * jnp.bfloat16(C6)
    high, low = split(C3 * n + (C4 * x + dot(x_high, mixed)))
    return dot(x_high, high) + dot(x_high, low)


def write_root(root_ref, frob, n, x, upper):
    scale = lax.rsqrt(jnp.sqrt(frob))
    total = (C1 * n + C2 * x) + upper
    root_ref[...] = (total * scale).astype(jnp.bfloat16)
    row = lax.broadcasted_iota(jnp.int32, (LANES, LANES), 0)
    col = lax.broadcasted_iota(jnp.int32, (LANES, LANES), 1)
    constant = jnp.where(row == col, C0, 0.0)
    for t in range(TILES):
        span = slice(t * LANES, (t + 1) * LANES)
        root_ref[span, span] = ((total[span, span] + constant) * scale).astype(jnp.bfloat16)


def refresh_kernel(
    block_ref, left_ref, right_ref, packed_ref, left_out, right_out,
    ordered, left_root, right_root
):
    for p in range(NX):
        for z in range(NZ):
            row = (z * NX + p) * PART
            ordered[row : row + PART, :] = block_ref[p * NZ + z]
    block = ordered[...]
    right = DECAY * right_ref[...] + ((1.0 - DECAY) / BS) * dot_tn(block, block)
    right_out[...] = right
    left = DECAY * left_ref[...] + ((1.0 - DECAY) / BS) * dot_nt(block, block)
    left_out[...] = left
    wide = block.astype(jnp.float32)
    grad_sq = jnp.sum(wide * wide, keepdims=True)
    right_frob, right_n = normalize(right)
    left_frob, left_n = normalize(left)
    right_high, right_x = square(right_n)
    left_high, left_x = square(left_n)
    right_upper = upper_terms(right_n, right_high, right_x)
    left_upper = upper_terms(left_n, left_high, left_x)
    write_root(right_root, right_frob, right_n, right_x, right_upper)
    half = dot(block, right_root[...]).astype(jnp.bfloat16)
    write_root(left_root, left_frob, left_n, left_x, left_upper)
    conditioned = dot(left_root[...], half)
    packed = conditioned.astype(jnp.bfloat16)
    for t in range(TILES):
        tile = packed[:, t * LANES : (t + 1) * LANES].reshape(NZ, NX, PART, LANES)
        for p in range(NX):
            packed_ref[p * NZ : (p + 1) * NZ, t * PART : (t + 1) * PART, :] = tile[:, p]
    line = lax.broadcasted_iota(jnp.int32, (EXTRA, LANES), 0)
    rest = jnp.where(line < 3, grad_sq, jnp.sum(conditioned * conditioned, keepdims=True))
    high = rest.astype(jnp.bfloat16).astype(jnp.float32)
    rest = rest - high
    middle = rest.astype(jnp.bfloat16).astype(jnp.float32)
    low = rest - middle
    kind = jnp.where(line < 3, line, line - 3)
    terms = jnp.where(kind == 0, high, jnp.where(kind == 1, middle, low)).astype(jnp.bfloat16)
    packed_ref[:, TILES * PART :, :] = jnp.broadcast_to(terms[None], (NX * NZ, EXTRA, LANES))


SMEM = functools.partial(pl.BlockSpec, memory_space=pltpu.SMEM)
VMEM = functools.partial(pl.BlockSpec, memory_space=pltpu.VMEM)
PARAMS = pltpu.CompilerParams(vmem_limit_bytes=VMEM_LIMIT)


def add_other(value, axis, partner):
    return value + lax.ppermute(value, axis, list(enumerate(partner)))


def body(gradient, owner, prev_left, prev_right):
    rows, cols = gradient.shape
    part = rows // NX
    place = lax.axis_index("x")
    table = jnp.clip(owner[0], 0, NX * NZ - 1)
    table = jnp.concatenate([table, jnp.roll(table, -place, axis=0)])
    f32, bf16 = jnp.float32, jnp.bfloat16

    spread = lax.all_to_all(gradient.reshape(NX, part, cols), "x", 0, 0, tiled=True)
    slots = pl.pallas_call(
        scatter_kernel,
        out_shape=jax.ShapeDtypeStruct((NX * NZ, part, BS), bf16),
        in_specs=[SMEM(), VMEM()],
        out_specs=VMEM(),
        compiler_params=PARAMS,
        name="scatter",
    )(table, spread)
    block = lax.all_to_all(slots, ("x", "z"), 0, 0, tiled=True)

    packed, left, right = pl.pallas_call(
        refresh_kernel,
        out_shape=[
            jax.ShapeDtypeStruct((NX * NZ, TILES * PART + EXTRA, LANES), bf16),
            jax.ShapeDtypeStruct((BS, BS), f32),
            jax.ShapeDtypeStruct((BS, BS), f32),
        ],
        in_specs=[VMEM()] * 3,
        out_specs=[VMEM()] * 3,
        scratch_shapes=[pltpu.VMEM((BS, BS), bf16)] * 3,
        compiler_params=PARAMS,
        name="refresh",
    )(block, prev_left[0, 0], prev_right[0, 0])

    returned = lax.all_to_all(packed, ("x", "z"), 0, 0, tiled=True)
    sums = pl.pallas_call(
        sums_kernel,
        out_shape=jax.ShapeDtypeStruct((8, LANES), f32),
        in_specs=[VMEM()],
        out_specs=VMEM(),
        compiler_params=PARAMS,
        name="sums",
    )(returned)
    sums = add_other(sums, "c", (1, 0))
    pieces = pl.pallas_call(
        gather_kernel,
        out_shape=[jax.ShapeDtypeStruct((part, cols), bf16)] * NX,
        in_specs=[SMEM(), pl.BlockSpec(memory_space=pl.ANY), VMEM()],
        out_specs=[VMEM()] * NX,
        compiler_params=PARAMS,
        name="gather",
    )(table, sums, returned)
    sums = add_other(add_other(sums, "y", (1, 0, 3, 2)), "y", (3, 2, 1, 0))
    moved = [pieces[0]] + [
        lax.ppermute(pieces[k], "x", [(i, (i + k) % NX) for i in range(NX)]) for k in range(1, NX)
    ]
    update = pl.pallas_call(
        finish_kernel,
        out_shape=jax.ShapeDtypeStruct((rows, cols), bf16),
        in_specs=[SMEM()] + [VMEM()] * (NX + 1),
        out_specs=VMEM(),
        compiler_params=PARAMS,
        name="finish",
    )(place.reshape(1, 1), sums, *moved)
    return update, left[None, None], right[None, None]


def solution(mesh):
    wide = Mesh(mesh.devices.reshape(NX, NZ, NT // 2, 2), ("x", "z", "y", "c"))
    dp, tensor = ("x", "z"), ("y", "c")
    return jax.shard_map(
        body,
        mesh=wide,
        in_specs=(
            P(dp, tensor),
            P(tensor, None, None),
            P(tensor, dp, None, None),
            P(tensor, dp, None, None),
        ),
        out_specs=(P(dp, tensor), P(tensor, dp, None, None), P(tensor, dp, None, None)),
        check_vma=False,
    )
```

time: 86.5 us -> 82.2 us (0.950); the launches traced: 84.8 us -> 81.9 us
  blocking collectives: 35 us -> 46.7 us
  waiting for transfers between devices: 19.9 us -> 13.7 us
  starting transfers between devices: 17.5 us -> 13.2 us
  Pallas kernels: 10.8 us -> 7.49 us
    all_to_all x2, blocking collectives: 35 us -> 46.7 us  [the longest x1 25.3 us: body(): block = lax.all_to_all(slots, ('x', 'z'), 0, 0, tiled=True)]
    all_to_all x2 -> x1, starting transfers between devices: 12.8 us -> 4.3 us  [body(): lax.all_to_all(gradient.reshape(NX, part, cols), 'x', 0, 0, tiled=True)]
    all_to_all x2 -> x1, waiting for transfers between devices: 14.9 us -> 8.68 us  [body(): lax.all_to_all(gradient.reshape(NX, part, cols), 'x', 0, 0, tiled=True)]
    ppermute x3 -> x6, starting transfers between devices: 4.7 us -> 8.94 us  [the longest x3 4.66 us: add_other(): return value + lax.ppermute(value, axis, list(enumerate(partner)))]
    pallas_call x1, Pallas kernels: 6.97 us -> 5.2 us  [body(): pl.pallas_call(refresh_kernel, out_shape=[jax.ShapeDtypeStruct((NX * NZ,...]
    ppermute x3 -> x6, waiting for transfers between devices: 4.97 us -> 5.01 us  [the longest x3 5 us: add_other(): return value + lax.ppermute(value, axis, list(enumerate(partner)))]
  transfers between devices with their start and end apart: 5 -> 7, of which waited for: 4 -> 4; matrix products, arithmetic and copies ran while one was open for 1% -> 0% of each run, Pallas kernels for 0% -> 0%
where the time goes in v3:
time: 82.2 us; the launch traced here: 81.9 us
  blocking collectives  46.7 us (57%)
  waiting for transfers between devices  13.7 us (17%)
  starting transfers between devices  13.2 us (16%)
  Pallas kernels  7.49 us (9%)
    all_to_all x1, blocking collectives, body(): block = lax.all_to_all(slots, ('x', 'z'), 0, 0, tiled=True)  25.3 us
    all_to_all x1, blocking collectives, body(): returned = lax.all_to_all(packed, ('x', 'z'), 0, 0, tiled=True)  21.4 us
    all_to_all x1, waiting for transfers between devices, body(): lax.all_to_all(gradient.reshape(NX, part, cols), 'x', 0, 0, tiled=True)  8.68 us
    pallas_call x1, Pallas kernels, body(): pl.pallas_call(refresh_kernel, out_shape=[jax.ShapeDtypeStruct((NX * NZ,...  5.2 us
    ppermute x3, waiting for transfers between devices, add_other(): return value + lax.ppermute(value, axis, list(enumerate(partner)))  5 us
    ppermute x3, starting transfers between devices, add_other(): return value + lax.ppermute(value, axis, list(enumerate(partner)))  4.66 us
    all_to_all x1, starting transfers between devices, body(): lax.all_to_all(gradient.reshape(NX, part, cols), 'x', 0, 0, tiled=True)  4.3 us
    ppermute x3, starting transfers between devices, body(): lax.ppermute(pieces[k], 'x', [(i, (i + k) % NX) for i in range(NX)])  4.27 us
  transfers between devices with their start and end apart: 7, of which 4 were waited for; matrix products, arithmetic and copies ran while one was open for 0% of the time, Pallas kernels for 0%

profile of v3, /device:TPU:32, one launch (start us, length us, event | category | flops | bytes accessed | tf_op | source)
XLA Modules:
  0.0 81.9 jit_solution(15315464693769570738)
XLA Ops:
  0.6 0.0 copy-start.2
  0.6 4.3 %all-to-all-start = ((bf16[4,16,3584]{2,1,0:T(8,128)(2,1)}), bf16[4,16,3584]{2,1,0:T(8,128)(2,1)S(1)}, u32[]{:S(2)}, u32[]{:S(2)}) async-start(bf16[4,16,3584]{2,1,0:T(8,128)(2,1)} %bitcast.10), calls=%async_computation | async-start | bytes 917504 | tf_op jit(solution)/shard_map/all_to_all | solution.py:171
  4.9 0.0 copy-done.2
  4.9 0.0 copy-start.1
  5.0 0.0 copy-start
  5.0 8.7 %all-to-all-done.rows_ref = bf16[4,16,3584]{2,1,0:T(8,128)(2,1)S(1)} async-done(((bf16[4,16,3584]{2,1,0:T(8,128)(2,1)}), bf16[4,16,3584]{2,1,0:T(8,128)(2,1)S(1)}, u32[]{:S(2)}, u32[]{:S(2)}) %all-to-all-start) | async-done | bytes 458784 | tf_op jit(solution)/shard_map/all_to_all | solution.py:171
  13.7 0.7 scatter.1
  14.4 25.3 %all_to_all.15.block_ref = bf16[32,16,512]{2,1,0:T(8,128)(2,1)S(1)} all-to-all(bf16[32,16,512]{2,1,0:T(8,128)(2,1)S(1)} %scatter.1), channel_id=1, replica_groups=mesh['x'=4,'z'=8,'y'=4,'c'=2] {'x','z'}, dimensions={0} | all-to-all | bytes 1048576 | tf_op jit(solution)/shard_map/all_to_all | solution.py:180
  39.7 0.0 copy-done.1
  39.7 0.0 copy-done
  39.7 5.2 %refresh.1 = (bf16[32,72,128]{2,1,0:T(8,128)(2,1)S(1)}, f32[512,512]{1,0:T(8,128)}, f32[512,512]{1,0:T(8,128)}) custom-call(bf16[32,16,512]{2,1,0:T(8,128)(2,1)S(1)} %all_to_all.15.block_ref, f32[512,512]{1,0:T(8,128)S(1)} %bitcast.8, f32[512,512]{1,0:T(8,128)S(1)} %bitcast.9), custom_call_target="tpu_custom_call" | custom-call | tf_op jit(solution)/shard_map/refresh/pallas_call | solution.py:182
  44.9 21.4 %all_to_all.16.slots_ref = bf16[32,72,128]{2,1,0:T(8,128)(2,1)S(1)} all-to-all(bf16[32,72,128]{2,1,0:T(8,128)(2,1)S(1)} %get-tuple-element.10), channel_id=1, replica_groups=mesh['x'=4,'z'=8,'y'=4,'c'=2] {'x','z'}, dimensions={0} | all-to-all | bytes 1179648 | tf_op jit(solution)/shard_map/all_to_all | solution.py:196
  66.4 0.1 collective-permute-start
  66.5 1.2 %collective-permute-done = f32[8,128]{1,0:T(8,128)S(1)} collective-permute-done((f32[8,128]{1,0:T(8,128)S(1)}, f32[8,128]{1,0:T(8,128)S(1)}, u32[]{:S(2)}, u32[]{:S(2)}) %collective-permute-start) | collective-permute-done | bytes 4128 | tf_op jit(solution)/shard_map/ppermute | solution.py:160
  67.6 0.7 gather.1
  68.3 0.7 collective-permute-start.3
  69.0 2.1 %collective-permute-start.4 = (bf16[16,3584]{1,0:T(8,128)(2,1)S(1)}, bf16[16,3584]{1,0:T(8,128)(2,1)S(1)}, u32[]{:S(2)}, u32[]{:S(2)}) collective-permute-start(bf16[16,3584]{1,0:T(8,128)(2,1)S(1)} %get-tuple-element.13), channel_id=1, source_target_pairs={{0,128},{64,192},{128,0},{192,64},{1,129},{65,193},{129,1},{193,65... | collective-permute-start | bytes 344072 | tf_op jit(solution)/shard_map/ppermute | solution.py:216
  71.1 1.4 %collective-permute-start.5 = (bf16[16,3584]{1,0:T(8,128)(2,1)S(1)}, bf16[16,3584]{1,0:T(8,128)(2,1)S(1)}, u32[]{:S(2)}, u32[]{:S(2)}) collective-permute-start(bf16[16,3584]{1,0:T(8,128)(2,1)S(1)} %get-tuple-element.14), channel_id=1, source_target_pairs={{0,192},{64,0},{128,64},{192,128},{1,193},{65,1},{129,65},{193,129... | collective-permute-start | bytes 344072 | tf_op jit(solution)/shard_map/ppermute | solution.py:216
  72.6 1.6 %collective-permute-start.1 = (f32[8,128]{1,0:T(8,128)S(1)}, f32[8,128]{1,0:T(8,128)S(1)}, u32[]{:S(2)}, u32[]{:S(2)}) collective-permute-start(f32[8,128]{1,0:T(8,128)S(1)} %add.21.after_ref), channel_id=1, source_target_pairs={{0,2},{2,0},{4,6},{6,4},{1,3},{3,1},{5,7},{7,5},{8,10},{10,8},{12,... | collective-permute-start | bytes 12296 | tf_op jit(solution)/shard_map/ppermute | solution.py:160
  74.1 2.0 %collective-permute-done.1 = f32[8,128]{1,0:T(8,128)S(1)} collective-permute-done((f32[8,128]{1,0:T(8,128)S(1)}, f32[8,128]{1,0:T(8,128)S(1)}, u32[]{:S(2)}, u32[]{:S(2)}) %collective-permute-start.1) | collective-permute-done | bytes 4128 | tf_op jit(solution)/shard_map/ppermute | solution.py:160
  76.2 3.0 %collective-permute-start.2 = (f32[8,128]{1,0:T(8,128)S(1)}, f32[8,128]{1,0:T(8,128)S(1)}, u32[]{:S(2)}, u32[]{:S(2)}) collective-permute-start(f32[8,128]{1,0:T(8,128)S(1)} %add.22), channel_id=1, source_target_pairs={{0,6},{2,4},{4,2},{6,0},{1,7},{3,5},{5,3},{7,1},{8,14},{10,12},{12... | collective-permute-start | bytes 12296 | tf_op jit(solution)/shard_map/ppermute | solution.py:160
  79.2 1.8 %collective-permute-done.2 = f32[8,128]{1,0:T(8,128)S(1)} collective-permute-done((f32[8,128]{1,0:T(8,128)S(1)}, f32[8,128]{1,0:T(8,128)S(1)}, u32[]{:S(2)}, u32[]{:S(2)}) %collective-permute-start.2) | collective-permute-done | bytes 4128 | tf_op jit(solution)/shard_map/ppermute | solution.py:160
  81.0 0.0 collective-permute-done.3.refs_1_
  81.0 0.0 collective-permute-done.4.refs_2_
  81.0 0.0 collective-permute-done.5.refs_3_
  81.0 0.9 %finish.1 = bf16[64,3584]{1,0:T(8,128)(2,1)} custom-call(s32[1,1]{1,0:T(1,128)} %bitcast.x_ref, f32[8,128]{1,0:T(8,128)S(1)} %add.23.sums_ref, bf16[16,3584]{1,0:T(8,128)(2,1)S(1)} %get-tuple-element.11.refs_0_, bf16[16,3584]{1,0:T(8,128)(2,1)S(1)} %collective-permute-done.3.refs_1_, bf16[16,3584]{1,0:T(8,128)(2,1)S(1)} %collective-permute-done.4.refs_2_, ...), custom_call_target="tpu_custom_call" | custom-call | tf_op jit(solution)/shard_map/finish/pallas_call | solution.py:218
  (8 shorter events, 0.1 us)
Async XLA Ops:
  0.6 4.3 %copy-start.2 = (s32[1,4,7]{2,1,0:T(4,128)S(1)}, s32[1,4,7]{2,1,0:T(4,128)}, u32[]{:S(2)}) copy-start(s32[1,4,7]{2,1,0:T(4,128)} %param.5) | copy-start | bytes 340
  0.6 13.1 %all-to-all-start = ((bf16[4,16,3584]{2,1,0:T(8,128)(2,1)}), bf16[4,16,3584]{2,1,0:T(8,128)(2,1)S(1)}, u32[]{:S(2)}, u32[]{:S(2)}) async-start(bf16[4,16,3584]{2,1,0:T(8,128)(2,1)} %bitcast.10), calls=%async_computation | async-start | bytes 917504 | tf_op jit(solution)/shard_map/all_to_all | solution.py:171
  4.9 34.7 %copy-start.1 = (f32[1,1,512,512]{3,2,1,0:T(8,128)S(1)}, f32[1,1,512,512]{3,2,1,0:T(8,128)}, u32[]{:S(2)}) copy-start(f32[1,1,512,512]{3,2,1,0:T(8,128)} %param.7) | copy-start | bytes 3145732
  5.0 34.7 %copy-start = (f32[1,1,512,512]{3,2,1,0:T(8,128)S(1)}, f32[1,1,512,512]{3,2,1,0:T(8,128)}, u32[]{:S(2)}) copy-start(f32[1,1,512,512]{3,2,1,0:T(8,128)} %param.6) | copy-start | bytes 3145732
  66.4 1.2 %collective-permute-start = (f32[8,128]{1,0:T(8,128)S(1)}, f32[8,128]{1,0:T(8,128)S(1)}, u32[]{:S(2)}, u32[]{:S(2)}) collective-permute-start(f32[8,128]{1,0:T(8,128)S(1)} %sums.1), channel_id=1, source_target_pairs={{0,1},{1,0},{2,3},{3,2},{4,5},{5,4},{6,7},{7,6},{8,9},{9,8},{10,11... | collective-permute-start | bytes 12296 | tf_op jit(solution)/shard_map/ppermute | solution.py:160
  68.3 12.7 %collective-permute-start.3 = (bf16[16,3584]{1,0:T(8,128)(2,1)S(1)}, bf16[16,3584]{1,0:T(8,128)(2,1)S(1)}, u32[]{:S(2)}, u32[]{:S(2)}) collective-permute-start(bf16[16,3584]{1,0:T(8,128)(2,1)S(1)} %get-tuple-element.12), channel_id=1, source_target_pairs={{0,64},{64,128},{128,192},{192,0},{1,65},{65,129},{129,193},{193,1... | collective-permute-start | bytes 344072 | tf_op jit(solution)/shard_map/ppermute | solution.py:216
  69.0 12.0 %collective-permute-start.4 = (bf16[16,3584]{1,0:T(8,128)(2,1)S(1)}, bf16[16,3584]{1,0:T(8,128)(2,1)S(1)}, u32[]{:S(2)}, u32[]{:S(2)}) collective-permute-start(bf16[16,3584]{1,0:T(8,128)(2,1)S(1)} %get-tuple-element.13), channel_id=1, source_target_pairs={{0,128},{64,192},{128,0},{192,64},{1,129},{65,193},{129,1},{193,65... | collective-permute-start | bytes 344072 | tf_op jit(solution)/shard_map/ppermute | solution.py:216
  71.1 9.9 %collective-permute-start.5 = (bf16[16,3584]{1,0:T(8,128)(2,1)S(1)}, bf16[16,3584]{1,0:T(8,128)(2,1)S(1)}, u32[]{:S(2)}, u32[]{:S(2)}) collective-permute-start(bf16[16,3584]{1,0:T(8,128)(2,1)S(1)} %get-tuple-element.14), channel_id=1, source_target_pairs={{0,192},{64,0},{128,64},{192,128},{1,193},{65,1},{129,65},{193,129... | collective-permute-start | bytes 344072 | tf_op jit(solution)/shard_map/ppermute | solution.py:216
  72.6 3.6 %collective-permute-start.1 = (f32[8,128]{1,0:T(8,128)S(1)}, f32[8,128]{1,0:T(8,128)S(1)}, u32[]{:S(2)}, u32[]{:S(2)}) collective-permute-start(f32[8,128]{1,0:T(8,128)S(1)} %add.21.after_ref), channel_id=1, source_target_pairs={{0,2},{2,0},{4,6},{6,4},{1,3},{3,1},{5,7},{7,5},{8,10},{10,8},{12,... | collective-permute-start | bytes 12296 | tf_op jit(solution)/shard_map/ppermute | solution.py:160
  76.2 4.8 %collective-permute-start.2 = (f32[8,128]{1,0:T(8,128)S(1)}, f32[8,128]{1,0:T(8,128)S(1)}, u32[]{:S(2)}, u32[]{:S(2)}) collective-permute-start(f32[8,128]{1,0:T(8,128)S(1)} %add.22), channel_id=1, source_target_pairs={{0,6},{2,4},{4,2},{6,0},{1,7},{3,5},{5,3},{7,1},{8,14},{10,12},{12... | collective-permute-start | bytes 12296 | tf_op jit(solution)/shard_map/ppermute | solution.py:160

commit v4 on v3

--- a/solution.py
+++ b/solution.py
@@ -42,9 +42,9 @@
     sums_ref[...] = jnp.where(line < 4, grad, cond)
 
 
-def gather_kernel(owner_ref, after_ref, slots_ref, *out_refs):
+def gather_kernel(turns, owner_ref, after_ref, slots_ref, *out_refs):
     del after_ref
-    for k, out_ref in enumerate(out_refs):
+    for k, out_ref in zip(turns, out_refs):
         for j in range(COLS):
             slot = owner_ref[NX + k, j]
             for t in range(TILES):
@@ -203,18 +203,25 @@
         name="sums",
     )(returned)
     sums = add_other(sums, "c", (1, 0))
-    pieces = pl.pallas_call(
-        gather_kernel,
-        out_shape=[jax.ShapeDtypeStruct((part, cols), bf16)] * NX,
-        in_specs=[SMEM(), pl.BlockSpec(memory_space=pl.ANY), VMEM()],
-        out_specs=[VMEM()] * NX,
-        compiler_params=PARAMS,
-        name="gather",
-    )(table, sums, returned)
-    sums = add_other(add_other(sums, "y", (1, 0, 3, 2)), "y", (3, 2, 1, 0))
-    moved = [pieces[0]] + [
-        lax.ppermute(pieces[k], "x", [(i, (i + k) % NX) for i in range(NX)]) for k in range(1, NX)
-    ]
+    def gather(turns, after):
+        return pl.pallas_call(
+            functools.partial(gather_kernel, turns),
+            out_shape=[jax.ShapeDtypeStruct((part, cols), bf16)] * len(turns),
+            in_specs=[SMEM(), pl.BlockSpec(memory_space=pl.ANY), VMEM()],
+            out_specs=[VMEM()] * len(turns),
+            compiler_params=PARAMS,
+            name="gather",
+        )(table, after, returned)
+
+    def turn(piece, k):
+        return lax.ppermute(piece, "x", [(i, (i + k) % NX) for i in range(NX)])
+
+    far, near = gather((2, 1), sums)
+    far, near = turn(far, 2), turn(near, 1)
+    sums = add_other(sums, "y", (1, 0, 3, 2))
+    last, own = gather((3, 0), sums)
+    moved = [own, near, far, turn(last, 3)]
+    sums = add_other(sums, "y", (3, 2, 1, 0))
     update = pl.pallas_call(
         finish_kernel,
         out_shape=jax.ShapeDtypeStruct((rows, cols), bf16),

time: 82.2 us -> 80.8 us (0.983)
  waiting for transfers between devices: 13.7 us -> 12.5 us
    ppermute x3, waiting for transfers between devices: 5 us -> 3.77 us  [add_other(): return value + lax.ppermute(value, axis, list(enumerate(partner)))]
  transfers between devices with their start and end apart: 7 -> 7, of which waited for: 4 -> 3; matrix products, arithmetic and copies ran while one was open for 0% -> 0% of each run, Pallas kernels for 0% -> 2%
where the time goes in v4:
time: 80.8 us; the launch traced here: 80.6 us
  blocking collectives  46.7 us (58%)
  starting transfers between devices  12.5 us (15%)
  waiting for transfers between devices  12.5 us (15%)
  Pallas kernels  8.1 us (10%)
    all_to_all x1, blocking collectives, body(): block = lax.all_to_all(slots, ('x', 'z'), 0, 0, tiled=True)  25.3 us
    all_to_all x1, blocking collectives, body(): returned = lax.all_to_all(packed, ('x', 'z'), 0, 0, tiled=True)  21.4 us
    all_to_all x1, waiting for transfers between devices, body(): lax.all_to_all(gradient.reshape(NX, part, cols), 'x', 0, 0, tiled=True)  8.68 us
    pallas_call x1, Pallas kernels, body(): pl.pallas_call(refresh_kernel, out_shape=[jax.ShapeDtypeStruct((NX * NZ,...  5.2 us
    ppermute x3, starting transfers between devices, turn(): return lax.ppermute(piece, 'x', [(i, (i + k) % NX) for i in range(NX)])  4.35 us
    all_to_all x1, starting transfers between devices, body(): lax.all_to_all(gradient.reshape(NX, part, cols), 'x', 0, 0, tiled=True)  4.3 us
    ppermute x3, starting transfers between devices, add_other(): return value + lax.ppermute(value, axis, list(enumerate(partner)))  3.85 us
    ppermute x3, waiting for transfers between devices, add_other(): return value + lax.ppermute(value, axis, list(enumerate(partner)))  3.77 us
  transfers between devices with their start and end apart: 7, of which 3 were waited for; matrix products, arithmetic and copies ran while one was open for 0% of the time, Pallas kernels for 2%

profile of v4, /device:TPU:32, one launch (start us, length us, event | category | flops | bytes accessed | tf_op | source)
XLA Modules:
  0.0 80.6 jit_solution(2455249076224665010)
XLA Ops:
  0.6 0.0 copy-start.2
  0.6 4.3 %all-to-all-start = ((bf16[4,16,3584]{2,1,0:T(8,128)(2,1)}), bf16[4,16,3584]{2,1,0:T(8,128)(2,1)S(1)}, u32[]{:S(2)}, u32[]{:S(2)}) async-start(bf16[4,16,3584]{2,1,0:T(8,128)(2,1)} %bitcast.10), calls=%async_computation | async-start | bytes 917504 | tf_op jit(solution)/shard_map/all_to_all | solution.py:171
  4.9 0.0 copy-done.2
  4.9 0.0 copy-start.1
  5.0 0.0 copy-start
  5.0 8.7 %all-to-all-done.rows_ref = bf16[4,16,3584]{2,1,0:T(8,128)(2,1)S(1)} async-done(((bf16[4,16,3584]{2,1,0:T(8,128)(2,1)}), bf16[4,16,3584]{2,1,0:T(8,128)(2,1)S(1)}, u32[]{:S(2)}, u32[]{:S(2)}) %all-to-all-start) | async-done | bytes 458784 | tf_op jit(solution)/shard_map/all_to_all | solution.py:171
  13.7 0.7 scatter.1
  14.4 25.3 %all_to_all.15.block_ref = bf16[32,16,512]{2,1,0:T(8,128)(2,1)S(1)} all-to-all(bf16[32,16,512]{2,1,0:T(8,128)(2,1)S(1)} %scatter.1), channel_id=1, replica_groups=mesh['x'=4,'z'=8,'y'=4,'c'=2] {'x','z'}, dimensions={0} | all-to-all | bytes 1048576 | tf_op jit(solution)/shard_map/all_to_all | solution.py:180
  39.7 0.0 copy-done.1
  39.7 0.0 copy-done
  39.7 5.2 %refresh.1 = (bf16[32,72,128]{2,1,0:T(8,128)(2,1)S(1)}, f32[512,512]{1,0:T(8,128)}, f32[512,512]{1,0:T(8,128)}) custom-call(bf16[32,16,512]{2,1,0:T(8,128)(2,1)S(1)} %all_to_all.15.block_ref, f32[512,512]{1,0:T(8,128)S(1)} %bitcast.8, f32[512,512]{1,0:T(8,128)S(1)} %bitcast.9), custom_call_target="tpu_custom_call" | custom-call | tf_op jit(solution)/shard_map/refresh/pallas_call | solution.py:182
  44.9 21.4 %all_to_all.16.slots_ref = bf16[32,72,128]{2,1,0:T(8,128)(2,1)S(1)} all-to-all(bf16[32,72,128]{2,1,0:T(8,128)(2,1)S(1)} %get-tuple-element.10), channel_id=1, replica_groups=mesh['x'=4,'z'=8,'y'=4,'c'=2] {'x','z'}, dimensions={0} | all-to-all | bytes 1179648 | tf_op jit(solution)/shard_map/all_to_all | solution.py:196
  66.4 0.1 collective-permute-start
  66.5 1.2 %collective-permute-done = f32[8,128]{1,0:T(8,128)S(1)} collective-permute-done((f32[8,128]{1,0:T(8,128)S(1)}, f32[8,128]{1,0:T(8,128)S(1)}, u32[]{:S(2)}, u32[]{:S(2)}) %collective-permute-start) | collective-permute-done | bytes 4128 | tf_op jit(solution)/shard_map/ppermute | solution.py:160
  67.6 1.6 %collective-permute-start.1 = (f32[8,128]{1,0:T(8,128)S(1)}, f32[8,128]{1,0:T(8,128)S(1)}, u32[]{:S(2)}, u32[]{:S(2)}) collective-permute-start(f32[8,128]{1,0:T(8,128)S(1)} %add.21.after_ref), channel_id=1, source_target_pairs={{0,2},{2,0},{4,6},{6,4},{1,3},{3,1},{5,7},{7,5},{8,10},{10,8},{12,... | collective-permute-start | bytes 12296 | tf_op jit(solution)/shard_map/ppermute | solution.py:160
  69.2 0.6 gather.3
  69.8 0.7 collective-permute-start.3
  70.5 2.2 %collective-permute-start.4 = (bf16[16,3584]{1,0:T(8,128)(2,1)S(1)}, bf16[16,3584]{1,0:T(8,128)(2,1)S(1)}, u32[]{:S(2)}, u32[]{:S(2)}) collective-permute-start(bf16[16,3584]{1,0:T(8,128)(2,1)S(1)} %get-tuple-element.13), channel_id=1, source_target_pairs={{0,128},{64,192},{128,0},{192,64},{1,129},{65,193},{129,1},{193,65... | collective-permute-start | bytes 344072 | tf_op jit(solution)/shard_map/ppermute | solution.py:217
  72.7 0.0 collective-permute-done.1
  72.7 0.6 gather.2
  73.3 1.5 %collective-permute-start.5 = (bf16[16,3584]{1,0:T(8,128)(2,1)S(1)}, bf16[16,3584]{1,0:T(8,128)(2,1)S(1)}, u32[]{:S(2)}, u32[]{:S(2)}) collective-permute-start(bf16[16,3584]{1,0:T(8,128)(2,1)S(1)} %get-tuple-element.14), channel_id=1, source_target_pairs={{0,192},{64,0},{128,64},{192,128},{1,193},{65,1},{129,65},{193,129... | collective-permute-start | bytes 344072 | tf_op jit(solution)/shard_map/ppermute | solution.py:217
  74.8 2.2 %collective-permute-start.2 = (f32[8,128]{1,0:T(8,128)S(1)}, f32[8,128]{1,0:T(8,128)S(1)}, u32[]{:S(2)}, u32[]{:S(2)}) collective-permute-start(f32[8,128]{1,0:T(8,128)S(1)} %add.22.after_ref), channel_id=1, source_target_pairs={{0,6},{2,4},{4,2},{6,0},{1,7},{3,5},{5,3},{7,1},{8,14},{10,12},{12... | collective-permute-start | bytes 12296 | tf_op jit(solution)/shard_map/ppermute | solution.py:160
  77.0 2.6 %collective-permute-done.2 = f32[8,128]{1,0:T(8,128)S(1)} collective-permute-done((f32[8,128]{1,0:T(8,128)S(1)}, f32[8,128]{1,0:T(8,128)S(1)}, u32[]{:S(2)}, u32[]{:S(2)}) %collective-permute-start.2) | collective-permute-done | bytes 4128 | tf_op jit(solution)/shard_map/ppermute | solution.py:160
  79.7 0.0 collective-permute-done.3.refs_1_
  79.7 0.0 collective-permute-done.4.refs_2_
  79.7 0.0 collective-permute-done.5.refs_3_
  79.7 0.9 %finish.1 = bf16[64,3584]{1,0:T(8,128)(2,1)} custom-call(s32[1,1]{1,0:T(1,128)} %bitcast.x_ref, f32[8,128]{1,0:T(8,128)S(1)} %add.23.sums_ref, bf16[16,3584]{1,0:T(8,128)(2,1)S(1)} %get-tuple-element.11.refs_0_, bf16[16,3584]{1,0:T(8,128)(2,1)S(1)} %collective-permute-done.3.refs_1_, bf16[16,3584]{1,0:T(8,128)(2,1)S(1)} %collective-permute-done.4.refs_2_, ...), custom_call_target="tpu_custom_call" | custom-call | tf_op jit(solution)/shard_map/finish/pallas_call | solution.py:225
  (8 shorter events, 0.1 us)
Async XLA Ops:
  0.6 4.3 %copy-start.2 = (s32[1,4,7]{2,1,0:T(4,128)S(1)}, s32[1,4,7]{2,1,0:T(4,128)}, u32[]{:S(2)}) copy-start(s32[1,4,7]{2,1,0:T(4,128)} %param.5) | copy-start | bytes 340
  0.6 13.1 %all-to-all-start = ((bf16[4,16,3584]{2,1,0:T(8,128)(2,1)}), bf16[4,16,3584]{2,1,0:T(8,128)(2,1)S(1)}, u32[]{:S(2)}, u32[]{:S(2)}) async-start(bf16[4,16,3584]{2,1,0:T(8,128)(2,1)} %bitcast.10), calls=%async_computation | async-start | bytes 917504 | tf_op jit(solution)/shard_map/all_to_all | solution.py:171
  4.9 34.7 %copy-start.1 = (f32[1,1,512,512]{3,2,1,0:T(8,128)S(1)}, f32[1,1,512,512]{3,2,1,0:T(8,128)}, u32[]{:S(2)}) copy-start(f32[1,1,512,512]{3,2,1,0:T(8,128)} %param.7) | copy-start | bytes 3145732
  5.0 34.7 %copy-start = (f32[1,1,512,512]{3,2,1,0:T(8,128)S(1)}, f32[1,1,512,512]{3,2,1,0:T(8,128)}, u32[]{:S(2)}) copy-start(f32[1,1,512,512]{3,2,1,0:T(8,128)} %param.6) | copy-start | bytes 3145732
  66.4 1.2 %collective-permute-start = (f32[8,128]{1,0:T(8,128)S(1)}, f32[8,128]{1,0:T(8,128)S(1)}, u32[]{:S(2)}, u32[]{:S(2)}) collective-permute-start(f32[8,128]{1,0:T(8,128)S(1)} %sums.1), channel_id=1, source_target_pairs={{0,1},{1,0},{2,3},{3,2},{4,5},{5,4},{6,7},{7,6},{8,9},{9,8},{10,11... | collective-permute-start | bytes 12296 | tf_op jit(solution)/shard_map/ppermute | solution.py:160
  67.6 5.1 %collective-permute-start.1 = (f32[8,128]{1,0:T(8,128)S(1)}, f32[8,128]{1,0:T(8,128)S(1)}, u32[]{:S(2)}, u32[]{:S(2)}) collective-permute-start(f32[8,128]{1,0:T(8,128)S(1)} %add.21.after_ref), channel_id=1, source_target_pairs={{0,2},{2,0},{4,6},{6,4},{1,3},{3,1},{5,7},{7,5},{8,10},{10,8},{12,... | collective-permute-start | bytes 12296 | tf_op jit(solution)/shard_map/ppermute | solution.py:160
  69.8 9.8 %collective-permute-start.3 = (bf16[16,3584]{1,0:T(8,128)(2,1)S(1)}, bf16[16,3584]{1,0:T(8,128)(2,1)S(1)}, u32[]{:S(2)}, u32[]{:S(2)}) collective-permute-start(bf16[16,3584]{1,0:T(8,128)(2,1)S(1)} %get-tuple-element.12), channel_id=1, source_target_pairs={{0,64},{64,128},{128,192},{192,0},{1,65},{65,129},{129,193},{193,1... | collective-permute-start | bytes 344072 | tf_op jit(solution)/shard_map/ppermute | solution.py:217
  70.5 9.2 %collective-permute-start.4 = (bf16[16,3584]{1,0:T(8,128)(2,1)S(1)}, bf16[16,3584]{1,0:T(8,128)(2,1)S(1)}, u32[]{:S(2)}, u32[]{:S(2)}) collective-permute-start(bf16[16,3584]{1,0:T(8,128)(2,1)S(1)} %get-tuple-element.13), channel_id=1, source_target_pairs={{0,128},{64,192},{128,0},{192,64},{1,129},{65,193},{129,1},{193,65... | collective-permute-start | bytes 344072 | tf_op jit(solution)/shard_map/ppermute | solution.py:217
  73.3 6.3 %collective-permute-start.5 = (bf16[16,3584]{1,0:T(8,128)(2,1)S(1)}, bf16[16,3584]{1,0:T(8,128)(2,1)S(1)}, u32[]{:S(2)}, u32[]{:S(2)}) collective-permute-start(bf16[16,3584]{1,0:T(8,128)(2,1)S(1)} %get-tuple-element.14), channel_id=1, source_target_pairs={{0,192},{64,0},{128,64},{192,128},{1,193},{65,1},{129,65},{193,129... | collective-permute-start | bytes 344072 | tf_op jit(solution)/shard_map/ppermute | solution.py:217
  74.8 4.8 %collective-permute-start.2 = (f32[8,128]{1,0:T(8,128)S(1)}, f32[8,128]{1,0:T(8,128)S(1)}, u32[]{:S(2)}, u32[]{:S(2)}) collective-permute-start(f32[8,128]{1,0:T(8,128)S(1)} %add.22.after_ref), channel_id=1, source_target_pairs={{0,6},{2,4},{4,2},{6,0},{1,7},{3,5},{5,3},{7,1},{8,14},{10,12},{12... | collective-permute-start | bytes 12296 | tf_op jit(solution)/shard_map/ppermute | solution.py:160

commit v5 on v4

--- a/solution.py
+++ b/solution.py
@@ -108,6 +108,10 @@
     for t in range(TILES):
         span = slice(t * LANES, (t + 1) * LANES)
         root_ref[span, span] = ((total[span, span] + constant) * scale).astype(jnp.bfloat16)
+
+
+def slot_at(x, z):
+    return (z & 1) * (NX * NZ // 2) + x * (NZ // 2) + (z >> 1)
 
 
 def refresh_kernel(
@@ -139,7 +143,8 @@
     for t in range(TILES):
         tile = packed[:, t * LANES : (t + 1) * LANES].reshape(NZ, NX, PART, LANES)
         for p in range(NX):
-            packed_ref[p * NZ : (p + 1) * NZ, t * PART : (t + 1) * PART, :] = tile[:, p]
+            for z in range(NZ):
+                packed_ref[slot_at(p, z), t * PART : (t + 1) * PART, :] = tile[z, p]
     line = lax.broadcasted_iota(jnp.int32, (EXTRA, LANES), 0)
     rest = jnp.where(line < 3, grad_sq, jnp.sum(conditioned * conditioned, keepdims=True))
     high = rest.astype(jnp.bfloat16).astype(jnp.float32)
@@ -165,7 +170,8 @@
     part = rows // NX
     place = lax.axis_index("x")
     table = jnp.clip(owner[0], 0, NX * NZ - 1)
-    table = jnp.concatenate([table, jnp.roll(table, -place, axis=0)])
+    slot = (table & 1) * (NX * NZ // 2) + (table // NZ) * (NZ // 2) + ((table & (NZ - 1)) >> 1)
+    table = jnp.concatenate([table, jnp.roll(slot, -place, axis=0)])
     f32, bf16 = jnp.float32, jnp.bfloat16
 
     spread = lax.all_to_all(gradient.reshape(NX, part, cols), "x", 0, 0, tiled=True)
@@ -177,7 +183,7 @@
         compiler_params=PARAMS,
         name="scatter",
     )(table, spread)
-    block = lax.all_to_all(slots, ("x", "z"), 0, 0, tiled=True)
+    block = lax.all_to_all(slots, ("x", "zh", "zl"), 0, 0, tiled=True)
 
     packed, left, right = pl.pallas_call(
         refresh_kernel,
@@ -193,7 +199,7 @@
         name="refresh",
     )(block, prev_left[0, 0], prev_right[0, 0])
 
-    returned = lax.all_to_all(packed, ("x", "z"), 0, 0, tiled=True)
+    returned = lax.all_to_all(packed, ("zl", "x", "zh"), 0, 0, tiled=True)
     sums = pl.pallas_call(
         sums_kernel,
         out_shape=jax.ShapeDtypeStruct((8, LANES), f32),
@@ -234,8 +240,8 @@
 
 
 def solution(mesh):
-    wide = Mesh(mesh.devices.reshape(NX, NZ, NT // 2, 2), ("x", "z", "y", "c"))
-    dp, tensor = ("x", "z"), ("y", "c")
+    wide = Mesh(mesh.devices.reshape(NX, NZ // 2, 2, NT // 2, 2), ("x", "zh", "zl", "y", "c"))
+    dp, tensor = ("x", "zh", "zl"), ("y", "c")
     return jax.shard_map(
         body,
         mesh=wide,

time: 80.8 us -> 80.2 us (level)
  blocking collectives: 46.7 us -> 45.1 us
  starting transfers between devices: 12.5 us -> 13.4 us
    all_to_all x2, blocking collectives: 46.7 us -> 45.1 us  [the longest x1 25.3 us: body(): block = lax.all_to_all(slots, ('x', 'zh', 'zl'), 0, 0, tiled=True)]
    ppermute x3, starting transfers between devices: 4.35 us -> 5.3 us  [turn(): return lax.ppermute(piece, 'x', [(i, (i + k) % NX) for i in range(NX)])]
where the time goes in v5:
time: 80.2 us; the launch traced here: 79.9 us
  blocking collectives  45.1 us (56%)
  starting transfers between devices  13.4 us (17%)
  waiting for transfers between devices  11.8 us (15%)
  Pallas kernels  8.1 us (10%)
    all_to_all x1, blocking collectives, body(): block = lax.all_to_all(slots, ('x', 'zh', 'zl'), 0, 0, tiled=True)  25.3 us
    all_to_all x1, blocking collectives, body(): returned = lax.all_to_all(packed, ('zl', 'x', 'zh'), 0, 0, tiled=True)  19.8 us
    all_to_all x1, waiting for transfers between devices, body(): lax.all_to_all(gradient.reshape(NX, part, cols), 'x', 0, 0, tiled=True)  8.01 us
    ppermute x3, starting transfers between devices, turn(): return lax.ppermute(piece, 'x', [(i, (i + k) % NX) for i in range(NX)])  5.3 us
    pallas_call x1, Pallas kernels, body(): pl.pallas_call(refresh_kernel, out_shape=[jax.ShapeDtypeStruct((NX * NZ,...  5.2 us
    all_to_all x1, starting transfers between devices, body(): lax.all_to_all(gradient.reshape(NX, part, cols), 'x', 0, 0, tiled=True)  4.3 us
    ppermute x3, starting transfers between devices, add_other(): return value + lax.ppermute(value, axis, list(enumerate(partner)))  3.84 us
    ppermute x3, waiting for transfers between devices, add_other(): return value + lax.ppermute(value, axis, list(enumerate(partner)))  3.8 us
  transfers between devices with their start and end apart: 7, of which 3 were waited for; matrix products, arithmetic and copies ran while one was open for 0% of the time, Pallas kernels for 2%

profile of v5, /device:TPU:32, one launch (start us, length us, event | category | flops | bytes accessed | tf_op | source)
XLA Modules:
  0.0 79.9 jit_solution(3305727699473113013)
XLA Ops:
  0.6 4.3 %all-to-all-start = ((bf16[4,16,3584]{2,1,0:T(8,128)(2,1)}), bf16[4,16,3584]{2,1,0:T(8,128)(2,1)S(1)}, u32[]{:S(2)}, u32[]{:S(2)}) async-start(bf16[4,16,3584]{2,1,0:T(8,128)(2,1)} %bitcast.12), calls=%async_computation | async-start | bytes 917504 | tf_op jit(solution)/shard_map/all_to_all | solution.py:177
  4.9 0.0 copy-start.2
  4.9 0.0 copy-start.1
  4.9 0.0 copy-start
  5.0 0.7 copy-done.2
  5.7 8.0 %all-to-all-done.rows_ref = bf16[4,16,3584]{2,1,0:T(8,128)(2,1)S(1)} async-done(((bf16[4,16,3584]{2,1,0:T(8,128)(2,1)}), bf16[4,16,3584]{2,1,0:T(8,128)(2,1)S(1)}, u32[]{:S(2)}, u32[]{:S(2)}) %all-to-all-start) | async-done | bytes 458784 | tf_op jit(solution)/shard_map/all_to_all | solution.py:177
  13.7 0.7 scatter.1
  14.4 25.3 %all_to_all.15.block_ref = bf16[32,16,512]{2,1,0:T(8,128)(2,1)S(1)} all-to-all(bf16[32,16,512]{2,1,0:T(8,128)(2,1)S(1)} %scatter.1), channel_id=1, replica_groups=mesh['x'=4,'zh'=4,'zl'=2,'y'=4,'c'=2] {'x','zh','zl'}, dimensions={0} | all-to-all | bytes 1048576 | tf_op jit(solution)/shard_map/all_to_all | solution.py:186
  39.7 0.0 copy-done.1
  39.7 0.0 copy-done
  39.7 5.2 %refresh.1 = (bf16[32,72,128]{2,1,0:T(8,128)(2,1)S(1)}, f32[512,512]{1,0:T(8,128)}, f32[512,512]{1,0:T(8,128)}) custom-call(bf16[32,16,512]{2,1,0:T(8,128)(2,1)S(1)} %all_to_all.15.block_ref, f32[512,512]{1,0:T(8,128)S(1)} %bitcast.10, f32[512,512]{1,0:T(8,128)S(1)} %bitcast.11), custom_call_target="tpu_custom_call" | custom-call | tf_op jit(solution)/shard_map/refresh/pallas_call | solution.py:188
  44.9 19.8 %all_to_all.16.slots_ref = bf16[32,72,128]{2,1,0:T(8,128)(2,1)S(1)} all-to-all(bf16[32,72,128]{2,1,0:T(8,128)(2,1)S(1)} %get-tuple-element.10), channel_id=1, replica_groups=mesh['x'=4,'zh'=4,'zl'=2,'y'=4,'c'=2] {'zl','x','zh'}, dimensions={0} | all-to-all | bytes 1179648 | tf_op jit(solution)/shard_map/all_to_all | solution.py:202
  64.8 0.1 collective-permute-start
  64.9 1.2 %collective-permute-done = f32[8,128]{1,0:T(8,128)S(1)} collective-permute-done((f32[8,128]{1,0:T(8,128)S(1)}, f32[8,128]{1,0:T(8,128)S(1)}, u32[]{:S(2)}, u32[]{:S(2)}) %collective-permute-start) | collective-permute-done | bytes 4128 | tf_op jit(solution)/shard_map/ppermute | solution.py:165
  66.0 1.6 %collective-permute-start.1 = (f32[8,128]{1,0:T(8,128)S(1)}, f32[8,128]{1,0:T(8,128)S(1)}, u32[]{:S(2)}, u32[]{:S(2)}) collective-permute-start(f32[8,128]{1,0:T(8,128)S(1)} %add.30.after_ref), channel_id=1, source_target_pairs={{0,2},{2,0},{4,6},{6,4},{1,3},{3,1},{5,7},{7,5},{8,10},{10,8},{12,... | collective-permute-start | bytes 12296 | tf_op jit(solution)/shard_map/ppermute | solution.py:165
  67.6 0.6 gather.3
  68.2 1.3 %collective-permute-start.3 = (bf16[16,3584]{1,0:T(8,128)(2,1)S(1)}, bf16[16,3584]{1,0:T(8,128)(2,1)S(1)}, u32[]{:S(2)}, u32[]{:S(2)}) collective-permute-start(bf16[16,3584]{1,0:T(8,128)(2,1)S(1)} %get-tuple-element.12), channel_id=1, source_target_pairs={{0,64},{64,128},{128,192},{192,0},{1,65},{65,129},{129,193},{193,1... | collective-permute-start | bytes 344072 | tf_op jit(solution)/shard_map/ppermute | solution.py:223
  69.5 2.6 %collective-permute-start.4 = (bf16[16,3584]{1,0:T(8,128)(2,1)S(1)}, bf16[16,3584]{1,0:T(8,128)(2,1)S(1)}, u32[]{:S(2)}, u32[]{:S(2)}) collective-permute-start(bf16[16,3584]{1,0:T(8,128)(2,1)S(1)} %get-tuple-element.13), channel_id=1, source_target_pairs={{0,128},{64,192},{128,0},{192,64},{1,129},{65,193},{129,1},{193,65... | collective-permute-start | bytes 344072 | tf_op jit(solution)/shard_map/ppermute | solution.py:223
  72.2 0.0 collective-permute-done.1
  72.2 0.6 gather.2
  72.8 1.4 %collective-permute-start.5 = (bf16[16,3584]{1,0:T(8,128)(2,1)S(1)}, bf16[16,3584]{1,0:T(8,128)(2,1)S(1)}, u32[]{:S(2)}, u32[]{:S(2)}) collective-permute-start(bf16[16,3584]{1,0:T(8,128)(2,1)S(1)} %get-tuple-element.14), channel_id=1, source_target_pairs={{0,192},{64,0},{128,64},{192,128},{1,193},{65,1},{129,65},{193,129... | collective-permute-start | bytes 344072 | tf_op jit(solution)/shard_map/ppermute | solution.py:223
  74.2 2.2 %collective-permute-start.2 = (f32[8,128]{1,0:T(8,128)S(1)}, f32[8,128]{1,0:T(8,128)S(1)}, u32[]{:S(2)}, u32[]{:S(2)}) collective-permute-start(f32[8,128]{1,0:T(8,128)S(1)} %add.31.after_ref), channel_id=1, source_target_pairs={{0,6},{2,4},{4,2},{6,0},{1,7},{3,5},{5,3},{7,1},{8,14},{10,12},{12... | collective-permute-start | bytes 12296 | tf_op jit(solution)/shard_map/ppermute | solution.py:165
  76.4 2.6 %collective-permute-done.2 = f32[8,128]{1,0:T(8,128)S(1)} collective-permute-done((f32[8,128]{1,0:T(8,128)S(1)}, f32[8,128]{1,0:T(8,128)S(1)}, u32[]{:S(2)}, u32[]{:S(2)}) %collective-permute-start.2) | collective-permute-done | bytes 4128 | tf_op jit(solution)/shard_map/ppermute | solution.py:165
  79.0 0.0 collective-permute-done.3.refs_1_
  79.0 0.0 collective-permute-done.4.refs_2_
  79.0 0.0 collective-permute-done.5.refs_3_
  79.0 0.9 %finish.1 = bf16[64,3584]{1,0:T(8,128)(2,1)} custom-call(s32[1,1]{1,0:T(1,128)} %bitcast.x_ref, f32[8,128]{1,0:T(8,128)S(1)} %add.32.sums_ref, bf16[16,3584]{1,0:T(8,128)(2,1)S(1)} %get-tuple-element.11.refs_0_, bf16[16,3584]{1,0:T(8,128)(2,1)S(1)} %collective-permute-done.3.refs_1_, bf16[16,3584]{1,0:T(8,128)(2,1)S(1)} %collective-permute-done.4.refs_2_, ...), custom_call_target="tpu_custom_call" | custom-call | tf_op jit(solution)/shard_map/finish/pallas_call | solution.py:231
  (9 shorter events, 0.1 us)
Async XLA Ops:
  0.6 13.1 %all-to-all-start = ((bf16[4,16,3584]{2,1,0:T(8,128)(2,1)}), bf16[4,16,3584]{2,1,0:T(8,128)(2,1)S(1)}, u32[]{:S(2)}, u32[]{:S(2)}) async-start(bf16[4,16,3584]{2,1,0:T(8,128)(2,1)} %bitcast.12), calls=%async_computation | async-start | bytes 917504 | tf_op jit(solution)/shard_map/all_to_all | solution.py:177
  4.9 0.7 copy-start.2
  4.9 34.7 %copy-start.1 = (f32[1,1,512,512]{3,2,1,0:T(8,128)S(1)}, f32[1,1,512,512]{3,2,1,0:T(8,128)}, u32[]{:S(2)}) copy-start(f32[1,1,512,512]{3,2,1,0:T(8,128)} %param.7) | copy-start | bytes 3145732
  4.9 34.7 %copy-start = (f32[1,1,512,512]{3,2,1,0:T(8,128)S(1)}, f32[1,1,512,512]{3,2,1,0:T(8,128)}, u32[]{:S(2)}) copy-start(f32[1,1,512,512]{3,2,1,0:T(8,128)} %param.6) | copy-start | bytes 3145732
  64.8 1.2 %collective-permute-start = (f32[8,128]{1,0:T(8,128)S(1)}, f32[8,128]{1,0:T(8,128)S(1)}, u32[]{:S(2)}, u32[]{:S(2)}) collective-permute-start(f32[8,128]{1,0:T(8,128)S(1)} %sums.1), channel_id=1, source_target_pairs={{0,1},{1,0},{2,3},{3,2},{4,5},{5,4},{6,7},{7,6},{8,9},{9,8},{10,11... | collective-permute-start | bytes 12296 | tf_op jit(solution)/shard_map/ppermute | solution.py:165
  66.0 6.2 %collective-permute-start.1 = (f32[8,128]{1,0:T(8,128)S(1)}, f32[8,128]{1,0:T(8,128)S(1)}, u32[]{:S(2)}, u32[]{:S(2)}) collective-permute-start(f32[8,128]{1,0:T(8,128)S(1)} %add.30.after_ref), channel_id=1, source_target_pairs={{0,2},{2,0},{4,6},{6,4},{1,3},{3,1},{5,7},{7,5},{8,10},{10,8},{12,... | collective-permute-start | bytes 12296 | tf_op jit(solution)/shard_map/ppermute | solution.py:165
  68.2 10.8 %collective-permute-start.3 = (bf16[16,3584]{1,0:T(8,128)(2,1)S(1)}, bf16[16,3584]{1,0:T(8,128)(2,1)S(1)}, u32[]{:S(2)}, u32[]{:S(2)}) collective-permute-start(bf16[16,3584]{1,0:T(8,128)(2,1)S(1)} %get-tuple-element.12), channel_id=1, source_target_pairs={{0,64},{64,128},{128,192},{192,0},{1,65},{65,129},{129,193},{193,1... | collective-permute-start | bytes 344072 | tf_op jit(solution)/shard_map/ppermute | solution.py:223
  69.5 9.5 %collective-permute-start.4 = (bf16[16,3584]{1,0:T(8,128)(2,1)S(1)}, bf16[16,3584]{1,0:T(8,128)(2,1)S(1)}, u32[]{:S(2)}, u32[]{:S(2)}) collective-permute-start(bf16[16,3584]{1,0:T(8,128)(2,1)S(1)} %get-tuple-element.13), channel_id=1, source_target_pairs={{0,128},{64,192},{128,0},{192,64},{1,129},{65,193},{129,1},{193,65... | collective-permute-start | bytes 344072 | tf_op jit(solution)/shard_map/ppermute | solution.py:223
  72.8 6.2 %collective-permute-start.5 = (bf16[16,3584]{1,0:T(8,128)(2,1)S(1)}, bf16[16,3584]{1,0:T(8,128)(2,1)S(1)}, u32[]{:S(2)}, u32[]{:S(2)}) collective-permute-start(bf16[16,3584]{1,0:T(8,128)(2,1)S(1)} %get-tuple-element.14), channel_id=1, source_target_pairs={{0,192},{64,0},{128,64},{192,128},{1,193},{65,1},{129,65},{193,129... | collective-permute-start | bytes 344072 | tf_op jit(solution)/shard_map/ppermute | solution.py:223
  74.2 4.8 %collective-permute-start.2 = (f32[8,128]{1,0:T(8,128)S(1)}, f32[8,128]{1,0:T(8,128)S(1)}, u32[]{:S(2)}, u32[]{:S(2)}) collective-permute-start(f32[8,128]{1,0:T(8,128)S(1)} %add.31.after_ref), channel_id=1, source_target_pairs={{0,6},{2,4},{4,2},{6,0},{1,7},{3,5},{5,3},{7,1},{8,14},{10,12},{12... | collective-permute-start | bytes 12296 | tf_op jit(solution)/shard_map/ppermute | solution.py:165

commit v6 on v5

--- a/solution.py
+++ b/solution.py
@@ -208,7 +208,6 @@
         compiler_params=PARAMS,
         name="sums",
     )(returned)
-    sums = add_other(sums, "c", (1, 0))
     def gather(turns, after):
         return pl.pallas_call(
             functools.partial(gather_kernel, turns),
@@ -222,10 +221,13 @@
     def turn(piece, k):
         return lax.ppermute(piece, "x", [(i, (i + k) % NX) for i in range(NX)])
 
-    far, near = gather((2, 1), sums)
-    far, near = turn(far, 2), turn(near, 1)
+    own, near, far, last = gather((0, 1, 2, 3), sums)
+    far = turn(far, 2)
+    sums = add_other(sums, "c", (1, 0))
+    near, sums = lax.optimization_barrier((near, sums))
+    near = turn(near, 1)
     sums = add_other(sums, "y", (1, 0, 3, 2))
-    last, own = gather((3, 0), sums)
+    last, sums = lax.optimization_barrier((last, sums))
     moved = [own, near, far, turn(last, 3)]
     sums = add_other(sums, "y", (3, 2, 1, 0))
     update = pl.pallas_call(

time: 80.2 us -> 79.5 us (level)
  transfers between devices with their start and end apart: 7 -> 7, of which waited for: 3 -> 3; matrix products, arithmetic and copies ran while one was open for 0% -> 0% of each run, Pallas kernels for 2% -> 1%
where the time goes in v6:
time: 79.5 us; the launch traced here: 79.1 us
  blocking collectives  45.1 us (57%)
  starting transfers between devices  13.9 us (17%)
  waiting for transfers between devices  11.1 us (14%)
  Pallas kernels  7.5 us (9%)
    all_to_all x1, blocking collectives, body(): block = lax.all_to_all(slots, ('x', 'zh', 'zl'), 0, 0, tiled=True)  25.3 us
    all_to_all x1, blocking collectives, body(): returned = lax.all_to_all(packed, ('zl', 'x', 'zh'), 0, 0, tiled=True)  19.8 us
    all_to_all x1, waiting for transfers between devices, body(): lax.all_to_all(gradient.reshape(NX, part, cols), 'x', 0, 0, tiled=True)  8.01 us
    ppermute x3, starting transfers between devices, turn(): return lax.ppermute(piece, 'x', [(i, (i + k) % NX) for i in range(NX)])  5.75 us
    pallas_call x1, Pallas kernels, body(): pl.pallas_call(refresh_kernel, out_shape=[jax.ShapeDtypeStruct((NX * NZ,...  5.2 us
    all_to_all x1, starting transfers between devices, body(): lax.all_to_all(gradient.reshape(NX, part, cols), 'x', 0, 0, tiled=True)  4.3 us
    ppermute x3, starting transfers between devices, add_other(): return value + lax.ppermute(value, axis, list(enumerate(partner)))  3.84 us
    ppermute x3, waiting for transfers between devices, add_other(): return value + lax.ppermute(value, axis, list(enumerate(partner)))  3.1 us
  transfers between devices with their start and end apart: 7, of which 3 were waited for; matrix products, arithmetic and copies ran while one was open for 0% of the time, Pallas kernels for 1%

profile of v6, /device:TPU:32, one launch (start us, length us, event | category | flops | bytes accessed | tf_op | source)
XLA Modules:
  0.0 79.1 jit_solution(5202583276987123625)
XLA Ops:
  0.6 4.3 %all-to-all-start = ((bf16[4,16,3584]{2,1,0:T(8,128)(2,1)}), bf16[4,16,3584]{2,1,0:T(8,128)(2,1)S(1)}, u32[]{:S(2)}, u32[]{:S(2)}) async-start(bf16[4,16,3584]{2,1,0:T(8,128)(2,1)} %bitcast.12), calls=%async_computation | async-start | bytes 917504 | tf_op jit(solution)/shard_map/all_to_all | solution.py:177
  4.9 0.0 copy-start.2
  4.9 0.0 copy-start.1
  4.9 0.0 copy-start
  5.0 0.7 copy-done.2
  5.7 8.0 %all-to-all-done.rows_ref = bf16[4,16,3584]{2,1,0:T(8,128)(2,1)S(1)} async-done(((bf16[4,16,3584]{2,1,0:T(8,128)(2,1)}), bf16[4,16,3584]{2,1,0:T(8,128)(2,1)S(1)}, u32[]{:S(2)}, u32[]{:S(2)}) %all-to-all-start) | async-done | bytes 458784 | tf_op jit(solution)/shard_map/all_to_all | solution.py:177
  13.7 0.7 scatter.1
  14.4 25.3 %all_to_all.15.block_ref = bf16[32,16,512]{2,1,0:T(8,128)(2,1)S(1)} all-to-all(bf16[32,16,512]{2,1,0:T(8,128)(2,1)S(1)} %scatter.1), channel_id=1, replica_groups=mesh['x'=4,'zh'=4,'zl'=2,'y'=4,'c'=2] {'x','zh','zl'}, dimensions={0} | all-to-all | bytes 1048576 | tf_op jit(solution)/shard_map/all_to_all | solution.py:186
  39.7 0.0 copy-done.1
  39.7 0.0 copy-done
  39.7 5.2 %refresh.1 = (bf16[32,72,128]{2,1,0:T(8,128)(2,1)S(1)}, f32[512,512]{1,0:T(8,128)}, f32[512,512]{1,0:T(8,128)}) custom-call(bf16[32,16,512]{2,1,0:T(8,128)(2,1)S(1)} %all_to_all.15.block_ref, f32[512,512]{1,0:T(8,128)S(1)} %bitcast.10, f32[512,512]{1,0:T(8,128)S(1)} %bitcast.11), custom_call_target="tpu_custom_call" | custom-call | tf_op jit(solution)/shard_map/refresh/pallas_call | solution.py:188
  44.9 19.8 %all_to_all.16.slots_ref = bf16[32,72,128]{2,1,0:T(8,128)(2,1)S(1)} all-to-all(bf16[32,72,128]{2,1,0:T(8,128)(2,1)S(1)} %get-tuple-element.14), channel_id=1, replica_groups=mesh['x'=4,'zh'=4,'zl'=2,'y'=4,'c'=2] {'zl','x','zh'}, dimensions={0} | all-to-all | bytes 1179648 | tf_op jit(solution)/shard_map/all_to_all | solution.py:202
  64.8 0.1 collective-permute-start
  64.9 0.7 gather.1
  65.6 0.5 collective-permute-done
  66.0 1.6 %collective-permute-start.1 = (f32[8,128]{1,0:T(8,128)S(1)}, f32[8,128]{1,0:T(8,128)S(1)}, u32[]{:S(2)}, u32[]{:S(2)}) collective-permute-start(f32[8,128]{1,0:T(8,128)S(1)} %add.30), channel_id=1, source_target_pairs={{0,2},{2,0},{4,6},{6,4},{1,3},{3,1},{5,7},{7,5},{8,10},{10,8},{12,... | collective-permute-start | bytes 12296 | tf_op jit(solution)/shard_map/ppermute | solution.py:165
  67.6 2.5 %collective-permute-start.4 = (bf16[16,3584]{1,0:T(8,128)(2,1)S(1)}, bf16[16,3584]{1,0:T(8,128)(2,1)S(1)}, u32[]{:S(2)}, u32[]{:S(2)}) collective-permute-start(bf16[16,3584]{1,0:T(8,128)(2,1)S(1)} %get-tuple-element.21), channel_id=1, source_target_pairs={{0,128},{64,192},{128,0},{192,64},{1,129},{65,193},{129,1},{193,65... | collective-permute-start | bytes 344072 | tf_op jit(solution)/shard_map/ppermute | solution.py:222
  70.1 0.7 collective-permute-start.3
  70.8 0.0 collective-permute-done.1
  70.9 2.5 %collective-permute-start.5 = (bf16[16,3584]{1,0:T(8,128)(2,1)S(1)}, bf16[16,3584]{1,0:T(8,128)(2,1)S(1)}, u32[]{:S(2)}, u32[]{:S(2)}) collective-permute-start(bf16[16,3584]{1,0:T(8,128)(2,1)S(1)} %get-tuple-element.22), channel_id=1, source_target_pairs={{0,192},{64,0},{128,64},{192,128},{1,193},{65,1},{129,65},{193,129... | collective-permute-start | bytes 344072 | tf_op jit(solution)/shard_map/ppermute | solution.py:222
  73.4 2.2 %collective-permute-start.2 = (f32[8,128]{1,0:T(8,128)S(1)}, f32[8,128]{1,0:T(8,128)S(1)}, u32[]{:S(2)}, u32[]{:S(2)}) collective-permute-start(f32[8,128]{1,0:T(8,128)S(1)} %add.31), channel_id=1, source_target_pairs={{0,6},{2,4},{4,2},{6,0},{1,7},{3,5},{5,3},{7,1},{8,14},{10,12},{12... | collective-permute-start | bytes 12296 | tf_op jit(solution)/shard_map/ppermute | solution.py:165
  75.5 2.6 %collective-permute-done.2 = f32[8,128]{1,0:T(8,128)S(1)} collective-permute-done((f32[8,128]{1,0:T(8,128)S(1)}, f32[8,128]{1,0:T(8,128)S(1)}, u32[]{:S(2)}, u32[]{:S(2)}) %collective-permute-start.2) | collective-permute-done | bytes 4128 | tf_op jit(solution)/shard_map/ppermute | solution.py:165
  78.2 0.0 collective-permute-done.4.refs_2_
  78.2 0.0 collective-permute-done.3.refs_1_
  78.2 0.0 collective-permute-done.5.refs_3_
  78.2 0.9 %finish.1 = bf16[64,3584]{1,0:T(8,128)(2,1)} custom-call(s32[1,1]{1,0:T(1,128)} %bitcast.x_ref, f32[8,128]{1,0:T(8,128)S(1)} %add.32.sums_ref, bf16[16,3584]{1,0:T(8,128)(2,1)S(1)} %get-tuple-element.19.refs_0_, bf16[16,3584]{1,0:T(8,128)(2,1)S(1)} %collective-permute-done.3.refs_1_, bf16[16,3584]{1,0:T(8,128)(2,1)S(1)} %collective-permute-done.4.refs_2_, ...), custom_call_target="tpu_custom_call" | custom-call | tf_op jit(solution)/shard_map/finish/pallas_call | solution.py:233
  (9 shorter events, 0.1 us)
Async XLA Ops:
  0.6 13.1 %all-to-all-start = ((bf16[4,16,3584]{2,1,0:T(8,128)(2,1)}), bf16[4,16,3584]{2,1,0:T(8,128)(2,1)S(1)}, u32[]{:S(2)}, u32[]{:S(2)}) async-start(bf16[4,16,3584]{2,1,0:T(8,128)(2,1)} %bitcast.12), calls=%async_computation | async-start | bytes 917504 | tf_op jit(solution)/shard_map/all_to_all | solution.py:177
  4.9 0.7 copy-start.2
  4.9 34.7 %copy-start.1 = (f32[1,1,512,512]{3,2,1,0:T(8,128)S(1)}, f32[1,1,512,512]{3,2,1,0:T(8,128)}, u32[]{:S(2)}) copy-start(f32[1,1,512,512]{3,2,1,0:T(8,128)} %param.7) | copy-start | bytes 3145732
  4.9 34.7 %copy-start = (f32[1,1,512,512]{3,2,1,0:T(8,128)S(1)}, f32[1,1,512,512]{3,2,1,0:T(8,128)}, u32[]{:S(2)}) copy-start(f32[1,1,512,512]{3,2,1,0:T(8,128)} %param.6) | copy-start | bytes 3145732
  64.8 1.2 %collective-permute-start = (f32[8,128]{1,0:T(8,128)S(1)}, f32[8,128]{1,0:T(8,128)S(1)}, u32[]{:S(2)}, u32[]{:S(2)}) collective-permute-start(f32[8,128]{1,0:T(8,128)S(1)} %sums.1.after_ref), channel_id=1, source_target_pairs={{0,1},{1,0},{2,3},{3,2},{4,5},{5,4},{6,7},{7,6},{8,9},{9,8},{10,11... | collective-permute-start | bytes 12296 | tf_op jit(solution)/shard_map/ppermute | solution.py:165
  66.0 4.8 %collective-permute-start.1 = (f32[8,128]{1,0:T(8,128)S(1)}, f32[8,128]{1,0:T(8,128)S(1)}, u32[]{:S(2)}, u32[]{:S(2)}) collective-permute-start(f32[8,128]{1,0:T(8,128)S(1)} %add.30), channel_id=1, source_target_pairs={{0,2},{2,0},{4,6},{6,4},{1,3},{3,1},{5,7},{7,5},{8,10},{10,8},{12,... | collective-permute-start | bytes 12296 | tf_op jit(solution)/shard_map/ppermute | solution.py:165
  67.6 10.6 %collective-permute-start.4 = (bf16[16,3584]{1,0:T(8,128)(2,1)S(1)}, bf16[16,3584]{1,0:T(8,128)(2,1)S(1)}, u32[]{:S(2)}, u32[]{:S(2)}) collective-permute-start(bf16[16,3584]{1,0:T(8,128)(2,1)S(1)} %get-tuple-element.21), channel_id=1, source_target_pairs={{0,128},{64,192},{128,0},{192,64},{1,129},{65,193},{129,1},{193,65... | collective-permute-start | bytes 344072 | tf_op jit(solution)/shard_map/ppermute | solution.py:222
  70.1 8.1 %collective-permute-start.3 = (bf16[16,3584]{1,0:T(8,128)(2,1)S(1)}, bf16[16,3584]{1,0:T(8,128)(2,1)S(1)}, u32[]{:S(2)}, u32[]{:S(2)}) collective-permute-start(bf16[16,3584]{1,0:T(8,128)(2,1)S(1)} %get-tuple-element.20), channel_id=1, source_target_pairs={{0,64},{64,128},{128,192},{192,0},{1,65},{65,129},{129,193},{193,1... | collective-permute-start | bytes 344072 | tf_op jit(solution)/shard_map/ppermute | solution.py:222
  70.9 7.3 %collective-permute-start.5 = (bf16[16,3584]{1,0:T(8,128)(2,1)S(1)}, bf16[16,3584]{1,0:T(8,128)(2,1)S(1)}, u32[]{:S(2)}, u32[]{:S(2)}) collective-permute-start(bf16[16,3584]{1,0:T(8,128)(2,1)S(1)} %get-tuple-element.22), channel_id=1, source_target_pairs={{0,192},{64,0},{128,64},{192,128},{1,193},{65,1},{129,65},{193,129... | collective-permute-start | bytes 344072 | tf_op jit(solution)/shard_map/ppermute | solution.py:222
  73.4 4.8 %collective-permute-start.2 = (f32[8,128]{1,0:T(8,128)S(1)}, f32[8,128]{1,0:T(8,128)S(1)}, u32[]{:S(2)}, u32[]{:S(2)}) collective-permute-start(f32[8,128]{1,0:T(8,128)S(1)} %add.31), channel_id=1, source_target_pairs={{0,6},{2,4},{4,2},{6,0},{1,7},{3,5},{5,3},{7,1},{8,14},{10,12},{12... | collective-permute-start | bytes 12296 | tf_op jit(solution)/shard_map/ppermute | solution.py:165

commit v7 on v6

--- a/solution.py
+++ b/solution.py
@@ -121,7 +121,7 @@
     for p in range(NX):
         for z in range(NZ):
             row = (z * NX + p) * PART
-            ordered[row : row + PART, :] = block_ref[p * NZ + z]
+            ordered[row : row + PART, :] = block_ref[slot_at(p, z)]
     block = ordered[...]
     right = DECAY * right_ref[...] + ((1.0 - DECAY) / BS) * dot_tn(block, block)
     right_out[...] = right
@@ -171,7 +171,7 @@
     place = lax.axis_index("x")
     table = jnp.clip(owner[0], 0, NX * NZ - 1)
     slot = (table & 1) * (NX * NZ // 2) + (table // NZ) * (NZ // 2) + ((table & (NZ - 1)) >> 1)
-    table = jnp.concatenate([table, jnp.roll(slot, -place, axis=0)])
+    table = jnp.concatenate([slot, jnp.roll(slot, -place, axis=0)])
     f32, bf16 = jnp.float32, jnp.bfloat16
 
     spread = lax.all_to_all(gradient.reshape(NX, part, cols), "x", 0, 0, tiled=True)
@@ -183,7 +183,7 @@
         compiler_params=PARAMS,
         name="scatter",
     )(table, spread)
-    block = lax.all_to_all(slots, ("x", "zh", "zl"), 0, 0, tiled=True)
+    block = lax.all_to_all(slots, ("zl", "x", "zh"), 0, 0, tiled=True)
 
     packed, left, right = pl.pallas_call(
         refresh_kernel,

time: 79.5 us -> 79.3 us (level)
    all_to_all x1, blocking collectives: 25.3 us -> 23.9 us  [body(): block = lax.all_to_all(slots, ('zl', 'x', 'zh'), 0, 0, tiled=True)]
    all_to_all x1, blocking collectives: 19.8 us -> 21.2 us  [body(): returned = lax.all_to_all(packed, ('zl', 'x', 'zh'), 0, 0, tiled=True)]
where the time goes in v7:
time: 79.3 us; the launch traced here: 79 us
  blocking collectives  45 us (57%)
  starting transfers between devices  13.9 us (18%)
  waiting for transfers between devices  11.8 us (15%)
  Pallas kernels  7.49 us (9%)
    all_to_all x1, blocking collectives, body(): block = lax.all_to_all(slots, ('zl', 'x', 'zh'), 0, 0, tiled=True)  23.9 us
    all_to_all x1, blocking collectives, body(): returned = lax.all_to_all(packed, ('zl', 'x', 'zh'), 0, 0, tiled=True)  21.2 us
    all_to_all x1, waiting for transfers between devices, body(): lax.all_to_all(gradient.reshape(NX, part, cols), 'x', 0, 0, tiled=True)  8.67 us
    ppermute x3, starting transfers between devices, turn(): return lax.ppermute(piece, 'x', [(i, (i + k) % NX) for i in range(NX)])  5.75 us
    pallas_call x1, Pallas kernels, body(): pl.pallas_call(refresh_kernel, out_shape=[jax.ShapeDtypeStruct((NX * NZ,...  5.2 us
    all_to_all x1, starting transfers between devices, body(): lax.all_to_all(gradient.reshape(NX, part, cols), 'x', 0, 0, tiled=True)  4.3 us
    ppermute x3, starting transfers between devices, add_other(): return value + lax.ppermute(value, axis, list(enumerate(partner)))  3.84 us
    ppermute x3, waiting for transfers between devices, add_other(): return value + lax.ppermute(value, axis, list(enumerate(partner)))  3.1 us
  transfers between devices with their start and end apart: 7, of which 3 were waited for; matrix products, arithmetic and copies ran while one was open for 0% of the time, Pallas kernels for 1%

profile of v7, /device:TPU:32, one launch (start us, length us, event | category | flops | bytes accessed | tf_op | source)
XLA Modules:
  0.0 79.0 jit_solution(3986906519440698476)
XLA Ops:
  0.6 0.0 copy-start.2
  0.6 4.3 %all-to-all-start = ((bf16[4,16,3584]{2,1,0:T(8,128)(2,1)}), bf16[4,16,3584]{2,1,0:T(8,128)(2,1)S(1)}, u32[]{:S(2)}, u32[]{:S(2)}) async-start(bf16[4,16,3584]{2,1,0:T(8,128)(2,1)} %bitcast.34), calls=%async_computation | async-start | bytes 917504 | tf_op jit(solution)/shard_map/all_to_all | solution.py:177
  4.9 0.0 copy-done.2
  4.9 0.0 copy-start.1
  5.0 0.0 copy-start
  5.1 8.7 %all-to-all-done.rows_ref = bf16[4,16,3584]{2,1,0:T(8,128)(2,1)S(1)} async-done(((bf16[4,16,3584]{2,1,0:T(8,128)(2,1)}), bf16[4,16,3584]{2,1,0:T(8,128)(2,1)S(1)}, u32[]{:S(2)}, u32[]{:S(2)}) %all-to-all-start) | async-done | bytes 458784 | tf_op jit(solution)/shard_map/all_to_all | solution.py:177
  13.7 0.7 scatter.1
  14.4 23.9 %all_to_all.15.block_ref = bf16[32,16,512]{2,1,0:T(8,128)(2,1)S(1)} all-to-all(bf16[32,16,512]{2,1,0:T(8,128)(2,1)S(1)} %scatter.1), channel_id=1, replica_groups=mesh['x'=4,'zh'=4,'zl'=2,'y'=4,'c'=2] {'zl','x','zh'}, dimensions={0} | all-to-all | bytes 1048576 | tf_op jit(solution)/shard_map/all_to_all | solution.py:186
  38.3 0.0 copy-done.1
  38.3 0.0 copy-done
  38.3 5.2 %refresh.1 = (bf16[32,72,128]{2,1,0:T(8,128)(2,1)S(1)}, f32[512,512]{1,0:T(8,128)}, f32[512,512]{1,0:T(8,128)}) custom-call(bf16[32,16,512]{2,1,0:T(8,128)(2,1)S(1)} %all_to_all.15.block_ref, f32[512,512]{1,0:T(8,128)S(1)} %bitcast.32, f32[512,512]{1,0:T(8,128)S(1)} %bitcast.33), custom_call_target="tpu_custom_call" | custom-call | tf_op jit(solution)/shard_map/refresh/pallas_call | solution.py:188
  43.5 21.2 %all_to_all.16.slots_ref = bf16[32,72,128]{2,1,0:T(8,128)(2,1)S(1)} all-to-all(bf16[32,72,128]{2,1,0:T(8,128)(2,1)S(1)} %get-tuple-element.14), channel_id=1, replica_groups=mesh['x'=4,'zh'=4,'zl'=2,'y'=4,'c'=2] {'zl','x','zh'}, dimensions={0} | all-to-all | bytes 1179648 | tf_op jit(solution)/shard_map/all_to_all | solution.py:202
  64.7 0.1 collective-permute-start
  64.8 0.7 gather.1
  65.5 0.5 collective-permute-done
  65.9 1.6 %collective-permute-start.1 = (f32[8,128]{1,0:T(8,128)S(1)}, f32[8,128]{1,0:T(8,128)S(1)}, u32[]{:S(2)}, u32[]{:S(2)}) collective-permute-start(f32[8,128]{1,0:T(8,128)S(1)} %add.30), channel_id=1, source_target_pairs={{0,2},{2,0},{4,6},{6,4},{1,3},{3,1},{5,7},{7,5},{8,10},{10,8},{12,... | collective-permute-start | bytes 12296 | tf_op jit(solution)/shard_map/ppermute | solution.py:165
  67.5 2.5 %collective-permute-start.4 = (bf16[16,3584]{1,0:T(8,128)(2,1)S(1)}, bf16[16,3584]{1,0:T(8,128)(2,1)S(1)}, u32[]{:S(2)}, u32[]{:S(2)}) collective-permute-start(bf16[16,3584]{1,0:T(8,128)(2,1)S(1)} %get-tuple-element.21), channel_id=1, source_target_pairs={{0,128},{64,192},{128,0},{192,64},{1,129},{65,193},{129,1},{193,65... | collective-permute-start | bytes 344072 | tf_op jit(solution)/shard_map/ppermute | solution.py:222
  70.0 0.8 %collective-permute-start.3 = (bf16[16,3584]{1,0:T(8,128)(2,1)S(1)}, bf16[16,3584]{1,0:T(8,128)(2,1)S(1)}, u32[]{:S(2)}, u32[]{:S(2)}) collective-permute-start(bf16[16,3584]{1,0:T(8,128)(2,1)S(1)} %get-tuple-element.20), channel_id=1, source_target_pairs={{0,64},{64,128},{128,192},{192,0},{1,65},{65,129},{129,193},{193,1... | collective-permute-start | bytes 344072 | tf_op jit(solution)/shard_map/ppermute | solution.py:222
  70.9 0.0 collective-permute-done.1
  70.9 2.4 %collective-permute-start.5 = (bf16[16,3584]{1,0:T(8,128)(2,1)S(1)}, bf16[16,3584]{1,0:T(8,128)(2,1)S(1)}, u32[]{:S(2)}, u32[]{:S(2)}) collective-permute-start(bf16[16,3584]{1,0:T(8,128)(2,1)S(1)} %get-tuple-element.22), channel_id=1, source_target_pairs={{0,192},{64,0},{128,64},{192,128},{1,193},{65,1},{129,65},{193,129... | collective-permute-start | bytes 344072 | tf_op jit(solution)/shard_map/ppermute | solution.py:222
  73.3 2.2 %collective-permute-start.2 = (f32[8,128]{1,0:T(8,128)S(1)}, f32[8,128]{1,0:T(8,128)S(1)}, u32[]{:S(2)}, u32[]{:S(2)}) collective-permute-start(f32[8,128]{1,0:T(8,128)S(1)} %add.31), channel_id=1, source_target_pairs={{0,6},{2,4},{4,2},{6,0},{1,7},{3,5},{5,3},{7,1},{8,14},{10,12},{12... | collective-permute-start | bytes 12296 | tf_op jit(solution)/shard_map/ppermute | solution.py:165
  75.5 2.6 %collective-permute-done.2 = f32[8,128]{1,0:T(8,128)S(1)} collective-permute-done((f32[8,128]{1,0:T(8,128)S(1)}, f32[8,128]{1,0:T(8,128)S(1)}, u32[]{:S(2)}, u32[]{:S(2)}) %collective-permute-start.2) | collective-permute-done | bytes 4128 | tf_op jit(solution)/shard_map/ppermute | solution.py:165
  78.1 0.0 collective-permute-done.4.refs_2_
  78.1 0.0 collective-permute-done.3.refs_1_
  78.1 0.0 collective-permute-done.5.refs_3_
  78.1 0.9 %finish.1 = bf16[64,3584]{1,0:T(8,128)(2,1)} custom-call(s32[1,1]{1,0:T(1,128)} %bitcast.x_ref, f32[8,128]{1,0:T(8,128)S(1)} %add.32.sums_ref, bf16[16,3584]{1,0:T(8,128)(2,1)S(1)} %get-tuple-element.19.refs_0_, bf16[16,3584]{1,0:T(8,128)(2,1)S(1)} %collective-permute-done.3.refs_1_, bf16[16,3584]{1,0:T(8,128)(2,1)S(1)} %collective-permute-done.4.refs_2_, ...), custom_call_target="tpu_custom_call" | custom-call | tf_op jit(solution)/shard_map/finish/pallas_call | solution.py:233
  (8 shorter events, 0.1 us)
Async XLA Ops:
  0.6 4.3 %copy-start.2 = (s32[1,4,7]{2,1,0:T(4,128)S(1)}, s32[1,4,7]{2,1,0:T(4,128)}, u32[]{:S(2)}) copy-start(s32[1,4,7]{2,1,0:T(4,128)} %param.5) | copy-start | bytes 340
  0.6 13.1 %all-to-all-start = ((bf16[4,16,3584]{2,1,0:T(8,128)(2,1)}), bf16[4,16,3584]{2,1,0:T(8,128)(2,1)S(1)}, u32[]{:S(2)}, u32[]{:S(2)}) async-start(bf16[4,16,3584]{2,1,0:T(8,128)(2,1)} %bitcast.34), calls=%async_computation | async-start | bytes 917504 | tf_op jit(solution)/shard_map/all_to_all | solution.py:177
  4.9 33.3 %copy-start.1 = (f32[1,1,512,512]{3,2,1,0:T(8,128)S(1)}, f32[1,1,512,512]{3,2,1,0:T(8,128)}, u32[]{:S(2)}) copy-start(f32[1,1,512,512]{3,2,1,0:T(8,128)} %param.7) | copy-start | bytes 3145732
  5.0 33.3 %copy-start = (f32[1,1,512,512]{3,2,1,0:T(8,128)S(1)}, f32[1,1,512,512]{3,2,1,0:T(8,128)}, u32[]{:S(2)}) copy-start(f32[1,1,512,512]{3,2,1,0:T(8,128)} %param.6) | copy-start | bytes 3145732
  64.7 1.2 %collective-permute-start = (f32[8,128]{1,0:T(8,128)S(1)}, f32[8,128]{1,0:T(8,128)S(1)}, u32[]{:S(2)}, u32[]{:S(2)}) collective-permute-start(f32[8,128]{1,0:T(8,128)S(1)} %sums.1.after_ref), channel_id=1, source_target_pairs={{0,1},{1,0},{2,3},{3,2},{4,5},{5,4},{6,7},{7,6},{8,9},{9,8},{10,11... | collective-permute-start | bytes 12296 | tf_op jit(solution)/shard_map/ppermute | solution.py:165
  65.9 4.9 %collective-permute-start.1 = (f32[8,128]{1,0:T(8,128)S(1)}, f32[8,128]{1,0:T(8,128)S(1)}, u32[]{:S(2)}, u32[]{:S(2)}) collective-permute-start(f32[8,128]{1,0:T(8,128)S(1)} %add.30), channel_id=1, source_target_pairs={{0,2},{2,0},{4,6},{6,4},{1,3},{3,1},{5,7},{7,5},{8,10},{10,8},{12,... | collective-permute-start | bytes 12296 | tf_op jit(solution)/shard_map/ppermute | solution.py:165
  67.5 10.6 %collective-permute-start.4 = (bf16[16,3584]{1,0:T(8,128)(2,1)S(1)}, bf16[16,3584]{1,0:T(8,128)(2,1)S(1)}, u32[]{:S(2)}, u32[]{:S(2)}) collective-permute-start(bf16[16,3584]{1,0:T(8,128)(2,1)S(1)} %get-tuple-element.21), channel_id=1, source_target_pairs={{0,128},{64,192},{128,0},{192,64},{1,129},{65,193},{129,1},{193,65... | collective-permute-start | bytes 344072 | tf_op jit(solution)/shard_map/ppermute | solution.py:222
  70.0 8.1 %collective-permute-start.3 = (bf16[16,3584]{1,0:T(8,128)(2,1)S(1)}, bf16[16,3584]{1,0:T(8,128)(2,1)S(1)}, u32[]{:S(2)}, u32[]{:S(2)}) collective-permute-start(bf16[16,3584]{1,0:T(8,128)(2,1)S(1)} %get-tuple-element.20), channel_id=1, source_target_pairs={{0,64},{64,128},{128,192},{192,0},{1,65},{65,129},{129,193},{193,1... | collective-permute-start | bytes 344072 | tf_op jit(solution)/shard_map/ppermute | solution.py:222
  70.9 7.2 %collective-permute-start.5 = (bf16[16,3584]{1,0:T(8,128)(2,1)S(1)}, bf16[16,3584]{1,0:T(8,128)(2,1)S(1)}, u32[]{:S(2)}, u32[]{:S(2)}) collective-permute-start(bf16[16,3584]{1,0:T(8,128)(2,1)S(1)} %get-tuple-element.22), channel_id=1, source_target_pairs={{0,192},{64,0},{128,64},{192,128},{1,193},{65,1},{129,65},{193,129... | collective-permute-start | bytes 344072 | tf_op jit(solution)/shard_map/ppermute | solution.py:222
  73.3 4.8 %collective-permute-start.2 = (f32[8,128]{1,0:T(8,128)S(1)}, f32[8,128]{1,0:T(8,128)S(1)}, u32[]{:S(2)}, u32[]{:S(2)}) collective-permute-start(f32[8,128]{1,0:T(8,128)S(1)} %add.31), channel_id=1, source_target_pairs={{0,6},{2,4},{4,2},{6,0},{1,7},{3,5},{5,3},{7,1},{8,14},{10,12},{12... | collective-permute-start | bytes 12296 | tf_op jit(solution)/shard_map/ppermute | solution.py:165
